TPU v7x, 256 devices: a whole 4x4x8 slice. The times are simulated.
256 devices in a mesh: seq: 128 (over y, z, x_lo, core), chan: 2 (over x_hi).
Axes of the slice: x: 4 (x_hi: 2, x_lo: 2; x = x_hi * 2 + x_lo), y: 4, z: 8, core: 2. Of those that a mesh axis runs over, the one named last changes fastest.
Arguments:
- inputs: bfloat16 [262144, 256], P('seq', 'chan'), may hold values from -6 to 6
- cotangent: bfloat16 [262144, 256], P('seq', 'chan'), may hold values from -18 to 18
- residues: float32 [16, 16], replicated, may hold values from -4 to 4
- decay_rates: float32 [16, 16], replicated, may hold values from 1.9073486e-06 to 0.0333333333
- skip_weight: float32 [256], P('chan'), may hold values from -4 to 4
Outputs:
- input_grad: bfloat16 [262144, 256], P('seq', 'chan')
- residue_grad: float32 [16, 16], replicated
- skip_grad: float32 [256], P('chan')
All inputs are finite; a program needn't handle non-finite values.
Results may differ from a plain program's by a relative error of at most 0.0012.
Values may be sent and summed in bfloat16 or wider, within the bound.
A program may use at most 64 MiB of HBM per device.

v0:
```python
import math

import jax
import jax.numpy as jnp
from jax import lax
from jax.sharding import PartitionSpec as P

GROUP = 16
BLOCK = 512
NG = 16


precise = lax.Precision.HIGHEST


def join_states(earlier, later):
    return (earlier[0] * later[0], later[1] + later[0] * earlier[1])


def block_work(packed):
    x_item, y_item, powers, tail_powers, coef_item = packed
    block_len = x_item.shape[0]
    filter_taps = jnp.dot(coef_item, powers, precision=precise)
    padded = jnp.concatenate([filter_taps, jnp.zeros((block_len,), jnp.float32)])
    repeated = jnp.tile(padded, block_len)[: block_len * (2 * block_len - 1)]
    toeplitz = repeated.reshape(block_len, 2 * block_len - 1)[:, :block_len]
    x_float = x_item.astype(jnp.float32)
    y_float = y_item.astype(jnp.float32)
    local_dx = jnp.dot(toeplitz, y_float, precision=precise)
    gram_matrix = jnp.dot(x_float, y_float.T, precision=precise)
    widened = jnp.concatenate(
        [gram_matrix, jnp.zeros((block_len, block_len - 1), jnp.float32)], axis=1
    )
    flattened = jnp.concatenate([widened.reshape(-1), jnp.zeros((block_len,), jnp.float32)])
    lag_sums = jnp.sum(flattened.reshape(block_len, 2 * block_len)[:, :block_len], axis=0)
    local_grad = jnp.dot(powers, lag_sums, precision=precise)
    summaries = jnp.dot(powers, y_float, precision=precise)
    tails_x = jnp.dot(tail_powers, x_float, precision=precise)
    return (local_dx, local_grad, summaries, tails_x)


def convolve_items(x_items, y_items, rate_items, coef_items, block_count, incoming_fn):
    block_len = x_items.shape[1]
    offsets = jnp.arange(block_len, dtype=jnp.float32)
    powers = jnp.exp(-rate_items[:, :, None] * offsets)
    tail_powers = jnp.exp(-rate_items[:, :, None] * (block_len - offsets))
    local_dx, local_grad, summaries, tails_x = lax.map(
        block_work, (x_items, y_items, powers, tail_powers, coef_items)
    )
    item_count, mode_count, col_count = summaries.shape
    per_block = col_count // block_count
    states = summaries.reshape(item_count, mode_count, block_count, per_block)
    step_decay = jnp.exp(-rate_items * block_len)[:, :, None]
    ordered = jnp.flip(jnp.moveaxis(states, 2, 0), 0)
    factors = jnp.broadcast_to(step_decay, ordered.shape)
    inclusive = lax.associative_scan(join_states, (factors, ordered))[1]
    inclusive = jnp.moveaxis(jnp.flip(inclusive, 0), 0, 2)
    device_decay = jnp.exp(-rate_items * (block_len * block_count))[:, :, None]
    incoming = incoming_fn(device_decay, inclusive[:, :, 0])
    remaining = (block_count - 1 - jnp.arange(block_count)).astype(jnp.float32)
    reach_decay = jnp.exp(-rate_items[:, :, None] * (block_len * remaining))[..., None]
    after_state = jnp.concatenate(
        [inclusive[:, :, 1:], jnp.zeros_like(inclusive[:, :, :1])], axis=2
    )
    after_state = (after_state + reach_decay * incoming[:, :, None, :]).reshape(
        item_count, mode_count, col_count
    )
    cross_dx = jnp.einsum(
        "ims,imc->isc", coef_items[:, :, None] * tail_powers, after_state, precision=precise
    )
    cross_grad = jnp.sum(tails_x * after_state, axis=2)
    return (local_dx + cross_dx, local_grad + cross_grad)


def no_carry(device_decay, device_total):
    return jnp.zeros_like(device_total)


def shards(inputs, cotangent, residues, decay_rates, skip_weight):
    tokens, width_dev = inputs.shape
    total_len = tokens * lax.axis_size("seq")
    mode_norm = jnp.sqrt(-jnp.expm1(-2.0 * decay_rates))
    mode_coefs = residues * mode_norm
    skip_partial = jnp.einsum(
        "tc,tc->c", inputs, cotangent, preferred_element_type=jnp.float32
    ) / math.sqrt(total_len)
    x_wide, y_wide = (
        lax.all_to_all(inputs, "seq", split_axis=1, concat_axis=0, tiled=True),
        lax.all_to_all(cotangent, "seq", split_axis=1, concat_axis=0, tiled=True),
    )
    chan_dev = x_wide.shape[1]
    full_blocks = total_len // BLOCK
    x_items = jnp.transpose(x_wide.reshape(full_blocks, BLOCK, chan_dev), (2, 1, 0))
    y_items = jnp.transpose(y_wide.reshape(full_blocks, BLOCK, chan_dev), (2, 1, 0))
    first_channel = lax.axis_index("seq") * chan_dev
    channel_ids = first_channel + jnp.arange(chan_dev, dtype=jnp.int32)
    selector = (channel_ids[:, None] % NG == jnp.arange(NG, dtype=jnp.int32)[None, :]).astype(
        jnp.float32
    )
    rate_items = jnp.dot(selector, decay_rates, precision=precise)
    coef_items = jnp.dot(selector, mode_coefs, precision=precise)
    skip_items = lax.dynamic_slice_in_dim(skip_weight, first_channel, chan_dev)
    mixed, grads = convolve_items(x_items, y_items, rate_items, coef_items, full_blocks, no_carry)
    dx_items = (mixed + skip_items[:, None, None] * y_items.astype(jnp.float32)).astype(
        jnp.bfloat16
    )
    dx_wide = jnp.transpose(dx_items, (2, 1, 0)).reshape(total_len, chan_dev)
    input_grad = lax.all_to_all(dx_wide, "seq", split_axis=0, concat_axis=1, tiled=True)
    group_grad = jnp.dot(selector.T, grads, precision=precise) * mode_norm
    group_grad = group_grad / math.sqrt(GROUP * total_len)
    group_grad, skip_grad = lax.psum((group_grad, skip_partial), "seq")
    group_grad = lax.psum(group_grad, "chan")
    return (input_grad, group_grad, skip_grad)


def solution(mesh):
    placed = (P("seq", "chan"), P("seq", "chan"), P(), P(), P("chan"))
    return jax.shard_map(
        shards,
        mesh=mesh,
        in_specs=placed,
        out_specs=(P("seq", "chan"), P(), P("chan")),
        check_vma=False,
    )
```

profile of v0, /device:TPU:4, one launch (start us, length us, event | category | flops | bytes accessed | tf_op | source)
XLA Modules:
  0.0 402.8 jit_solution(14199440599802911040)
XLA Ops:
  0.6 2.5 copy.48
  3.1 0.5 broadcast.329
  3.7 3.7 reduce.8
  7.3 1.2 reshape.387
  8.5 14.4 %all-to-all-start = ((bf16[128,2,1024]{2,1,0:T(2,128)(2,1)}), bf16[128,2,1024]{2,1,0:T(2,128)(2,1)S(1)}, u32[]{:S(2)}, u32[]{:S(2)}) async-start(bf16[128,2,1024]{2,1,0:T(2,128)(2,1)} %reshape.387), calls=%async_computation | async-start | bytes 1048576 | tf_op jit(solution)/shard_map/all_to_all | solution.py:89
  23.8 0.5 copy.65
  24.3 2.8 reshape.369
  27.2 0.9 copy.55
  28.2 3.7 reduce.10
  31.9 1.2 reshape.391
  33.0 0.6 dynamic_slice.21
  34.1 7.9 %all-to-all-done = bf16[128,2,1024]{2,1,0:T(2,128)(2,1)S(1)} async-done(((bf16[128,2,1024]{2,1,0:T(2,128)(2,1)}), bf16[128,2,1024]{2,1,0:T(2,128)(2,1)S(1)}, u32[]{:S(2)}, u32[]{:S(2)}) %all-to-all-start) | async-done | bytes 524320 | tf_op jit(solution)/shard_map/all_to_all | solution.py:89
  42.0 6.4 %all-to-all-start.2 = ((bf16[128,2,1024]{2,1,0:T(2,128)(2,1)}), bf16[128,2,1024]{2,1,0:T(2,128)(2,1)S(1)}, u32[]{:S(2)}, u32[]{:S(2)}) async-start(bf16[128,2,1024]{2,1,0:T(2,128)(2,1)} %reshape.391), calls=%async_computation.2 | async-start | bytes 1048576 | tf_op jit(solution)/shard_map/all_to_all | solution.py:88
  48.4 0.5 reshape.388
  48.9 3.0 bitcast_reduce_fusion.1
  51.9 1.1 reshape.370
  53.0 1.4 copy.49
  54.4 0.3 convolution_bitcast_fusion
  54.7 0.6 slice.220
  55.3 0.6 slice.223
  56.3 0.3 slice.228
  56.6 0.3 slice.230
  59.5 0.3 slice.226
  62.5 0.6 slice.217
  63.2 0.3 pad.74
  63.6 0.3 pad.73
  64.2 0.6 pad.75
  64.9 0.6 pad.76
  65.5 0.3 rev.5
  65.9 1.0 fusion.7
  66.9 1.7 fusion.3
  68.8 0.5 all_to_all.48
  69.4 3.7 reduce.9
  73.0 1.2 reshape.389
  74.2 12.9 %all-to-all-start.1 = ((bf16[128,2,1024]{2,1,0:T(2,128)(2,1)}), bf16[128,2,1024]{2,1,0:T(2,128)(2,1)}, u32[]{:S(2)}, u32[]{:S(2)}) async-start(bf16[128,2,1024]{2,1,0:T(2,128)(2,1)} %reshape.389), calls=%async_computation.1 | async-start | bytes 1048576 | tf_op jit(solution)/shard_map/all_to_all | solution.py:108
  87.2 0.5 reshape.392
  87.6 3.0 bitcast_reduce_fusion
  90.6 0.3 reshape.373
  90.9 0.5 fusion.11
  91.4 1.6 concatenate.49
  93.1 2.9 reshape.374
  96.0 1.5 concatenate.50
  97.5 1.7 reshape.375
  99.2 0.6 fusion.4
  100.2 289.8 %all-reduce.22 = (f32[16,16]{1,0:T(8,128)S(1)}, f32[128]{0:T(128)}) all-reduce(f32[16,16]{1,0:T(8,128)S(1)} %multiply_multiply_fusion, f32[128]{0:T(128)S(1)} %broadcast_multiply_fusion.1), channel_id=1, replica_groups=mesh['seq'=128,'chan'=2] {'seq'}, use_global_device_ids=true, to_apply=%region_2.3 | all-reduce | flops 384 | bytes 3072 | tf_op jit(solution)/shard_map/psum | solution.py:111
  390.0 7.1 %psum.22 = f32[16,16]{1,0:T(8,128)} all-reduce(f32[16,16]{1,0:T(8,128)S(1)} %get-tuple-element.29), channel_id=1, replica_groups=mesh['seq'=128,'chan'=2] {'chan'}, use_global_device_ids=true, to_apply=%region_3.4 | all-reduce | flops 256 | bytes 2048 | tf_op jit(solution)/shard_map/psum | solution.py:112
  397.1 3.6 reshape.390
  400.7 1.9 copy.54
  (102 shorter events, 8.0 us)
Async XLA Ops:
  3.1 19.8 %copy-start.3 = (f32[16,16]{1,0:T(8,128)S(1)}, f32[16,16]{1,0:T(8,128)}, u32[]{:S(2)}) copy-start(f32[16,16]{1,0:T(8,128)} %param.8) | copy-start | bytes 3076
  3.1 20.0 %copy-start.4 = (f32[16,16]{1,0:T(8,128)S(1)}, f32[16,16]{1,0:T(8,128)}, u32[]{:S(2)}) copy-start(f32[16,16]{1,0:T(8,128)} %param.7) | copy-start | bytes 3076
  8.5 33.5 %all-to-all-start = ((bf16[128,2,1024]{2,1,0:T(2,128)(2,1)}), bf16[128,2,1024]{2,1,0:T(2,128)(2,1)S(1)}, u32[]{:S(2)}, u32[]{:S(2)}) async-start(bf16[128,2,1024]{2,1,0:T(2,128)(2,1)} %reshape.387), calls=%async_computation | async-start | bytes 1048576 | tf_op jit(solution)/shard_map/all_to_all | solution.py:89
  24.2 3.0 copy-start.2
  27.2 5.8 %copy-start.5 = (f32[128]{0:T(128)S(1)}, f32[128]{0:T(128)}, u32[]{:S(2)}) copy-start(f32[128]{0:T(128)} %param.9) | copy-start | bytes 1540
  27.2 6.4 %copy-start.1 = (bf16[2048,128]{1,0:T(8,128)(2,1)S(1)}, bf16[2048,128]{1,0:T(8,128)(2,1)}, u32[]{:S(2)}) copy-start(bf16[2048,128]{1,0:T(8,128)(2,1)} %param.6) | copy-start | bytes 1572868
  42.0 32.2 %all-to-all-start.2 = ((bf16[128,2,1024]{2,1,0:T(2,128)(2,1)}), bf16[128,2,1024]{2,1,0:T(2,128)(2,1)S(1)}, u32[]{:S(2)}, u32[]{:S(2)}) async-start(bf16[128,2,1024]{2,1,0:T(2,128)(2,1)} %reshape.391), calls=%async_computation.2 | async-start | bytes 1048576 | tf_op jit(solution)/shard_map/all_to_all | solution.py:88
  53.0 12.9 %copy-start = (f32[512,1023]{1,0:T(8,128)S(1)}, f32[512,1023]{1,0:T(8,128)}, u32[]{:S(2)}) copy-start(f32[512,1023]{1,0:T(8,128)} %reshape.369) | copy-start | bytes 6285316
  74.2 322.9 %all-to-all-start.1 = ((bf16[128,2,1024]{2,1,0:T(2,128)(2,1)}), bf16[128,2,1024]{2,1,0:T(2,128)(2,1)}, u32[]{:S(2)}, u32[]{:S(2)}) async-start(bf16[128,2,1024]{2,1,0:T(2,128)(2,1)} %reshape.389), calls=%async_computation.1 | async-start | bytes 1048576 | tf_op jit(solution)/shard_map/all_to_all | solution.py:108
where the time goes:
time: 408 us; the launch traced here: 403 us
  blocking collectives  297 us (73%)
  local copies, waits for them, and re-layouts  44.4 us (11%)
  starting transfers between devices  33.8 us (8%)
  other arithmetic  13.7 us (3%)
  waiting for transfers between devices  7.9 us (2%)
  matrix products  4.83 us (1%)
    psum x1, blocking collectives, shards(): group_grad, skip_grad = lax.psum((group_grad, skip_partial), 'seq')  290 us
    all_to_all x1, starting transfers between devices, shards(): lax.all_to_all(cotangent, 'seq', split_axis=1, concat_axis=0, tiled=True)  14.4 us
    all_to_all x1, starting transfers between devices, shards(): lax.all_to_all(dx_wide, 'seq', split_axis=0, concat_axis=1, tiled=True)  12.9 us
    unnamed x3, other arithmetic  11 us
    unnamed x22, local copies, waits for them, and re-layouts  9.43 us
  transfers between devices with their start and end apart: 3, of which 1 were waited for; matrix products, arithmetic and copies ran while one was open for 12% of the time, Pallas kernels for 0%

commit v1 on v0

v1 whole, which is shorter than its diff:
```python
import math

import jax
import jax.numpy as jnp
from jax import lax
from jax.experimental import pallas as pl
from jax.experimental.pallas import tpu as pltpu
from jax.sharding import PartitionSpec as P

MESH = pl.DeviceIdType.MESH
F32 = jnp.float32
BF16 = jnp.bfloat16
NG = 16
MODES = 16
GROUP = 16
TOK = 2048
CD = 128
BL = 128
NB = TOK // BL
NQ, NZ, NY = 4, 8, 4


def split(v):
    hi = v.astype(BF16)
    return hi, (v - hi.astype(F32)).astype(BF16)


def nn(a, b):
    return lax.dot_general(a, b, (((1,), (0,)), ((), ())), preferred_element_type=F32)


def nt(a, b):
    return lax.dot_general(a, b, (((1,), (1,)), ((), ())), preferred_element_type=F32)


def iota(shape, dim):
    return lax.broadcasted_iota(jnp.int32, shape, dim)


def fold(h):
    h = h + pltpu.roll(h, 64, 1)
    h = h + pltpu.roll(h, 32, 1)
    return h + pltpu.roll(h, 16, 1)


def pack(h):
    h = fold(h)
    keep = iota((8, CD), 1) // 16 == iota((8, CD), 0)
    first = jnp.sum(jnp.where(keep, h[:8], 0.0), axis=0, keepdims=True)
    second = jnp.sum(jnp.where(keep, h[8:], 0.0), axis=0, keepdims=True)
    row = iota((8, CD), 0)
    return jnp.where(row == 0, first, jnp.where(row == 1, second, 0.0))


def unpack(tile):
    keep = iota((8, CD), 1) // 16 == iota((8, CD), 0)
    return jnp.concatenate(
        [jnp.where(keep, tile[0:1], 0.0), jnp.where(keep, tile[1:2], 0.0)], axis=0
    )


def extract(full):
    group_of = iota((MODES, CD), 1) % NG
    out = jnp.zeros((MODES, CD), F32)
    for g in range(NG):
        out = out + jnp.where(group_of == g, full[MODES * g : MODES * (g + 1)], 0.0)
    return out


def suffix(load_s, count, w):
    acc = load_s(count - 1)
    for i in range(count - 2, -1, -1):
        acc = load_s(i) + w * acc
    return acc


def pairs(load_s, load_t, count, w):
    acc = load_t(0)
    total = None
    for i in range(1, count):
        term = acc * load_s(i)
        total = term if total is None else total + term
        acc = load_t(i) + w * acc
    return total, acc


def kernel(
    x_hbm, y_hbm, res_ref, dec_ref, skip_ref,
    dx_hbm, rg_ref, sg_ref,
    x, y, xg, yg, tmp, rmc_ref, cmc_ref, pw, pt, after, grow, ot, loc, qh, ql, outb, rowr,
    s1, t1, g1, s2, t2, g2, s3, m3,
    load_sem, out_sem, send_sem, recv_sem,
):
    me = lax.axis_index("seq")
    half = lax.axis_index("chan")
    q = lax.rem(me, NQ)
    z = lax.rem(me // NQ, NZ)
    yy = me // (NQ * NZ)

    def at(y_i, z_i, q_i, h_i):
        return {"seq": (y_i * NZ + z_i) * NQ + q_i, "chan": h_i}

    quad_peers = [at(yy, z, lax.rem(q + NQ - k, NQ), half) for k in range(1, NQ)]
    z_peers = [at(yy, lax.rem(z + NZ - k, NZ), q, half) for k in range(1, NZ)]
    y_peers = [at(lax.rem(yy + NY - k, NY), z, q, half) for k in range(1, NY)]
    o_peers = [at(lax.rem(yy + NY - k, NY), z, q, 1 - half) for k in range(NY)]

    load_y = pltpu.make_async_copy(y_hbm, y, load_sem.at[0])
    load_x = pltpu.make_async_copy(x_hbm, x, load_sem.at[1])
    load_y.start()
    load_x.start()
    barrier = pltpu.get_barrier_semaphore()
    everyone = quad_peers + z_peers + y_peers + o_peers
    for peer in everyone:
        pl.semaphore_signal(barrier, inc=1, device_id=peer, device_id_type=MESH)

    sent = []

    def send(buf, peers, first_slot, sem):
        copies = []
        for k, peer in enumerate(peers):
            slot = first_slot + k
            copy = pltpu.make_async_remote_copy(
                src_ref=buf.at[0],
                dst_ref=buf.at[slot],
                send_sem=send_sem.at[sem + k],
                recv_sem=recv_sem.at[sem + k],
                device_id=peer,
                device_id_type=MESH,
            )
            copy.start()
            copies.append(copy)
        sent.extend(copies)
        return copies

    def arrive(copies):
        for copy in copies:
            copy.wait_recv()

    rates = dec_ref[...]
    tmp[...] = jnp.zeros_like(tmp)
    for k in range(CD // NG):
        tmp[NG * k : NG * (k + 1), 0:MODES] = rates
    rmc = jnp.transpose(tmp[...])[:MODES]
    rmc_ref[...] = rmc
    span = 2 * BL
    ahead = iota((MODES, span), 1).astype(F32)
    behind = span - ahead
    for g in range(NG):
        column = jnp.broadcast_to(rmc[:, g : g + 1], (MODES, span))
        pw[MODES * g : MODES * (g + 1), :] = jnp.exp(-(column * ahead))
        pt[MODES * g : MODES * (g + 1), :] = jnp.exp(-(column * behind))

    step = pt[:, 0:1]
    wide = jnp.broadcast_to(step, (NG * MODES, 2 * CD))
    half_decay = jnp.exp(-(float(TOK // 2) * rmc))
    blocks = TOK // 2 // span

    def summary(ref, powers, order):
        hi, lo = split(powers[...])
        total = None
        for b in order:
            both = jnp.concatenate(
                [ref[b * span : (b + 1) * span, :], ref[TOK // 2 + b * span : TOK // 2 + (b + 1) * span, :]],
                axis=1,
            )
            part = nn(hi, both) + nn(lo, both)
            total = part if total is None else part + wide * total
        return extract(total[:, :CD]), extract(total[:, CD:])

    load_y.wait()
    first, second = summary(y, pw, range(blocks - 1, -1, -1))
    s1[0] = first + half_decay * second
    load_x.wait()
    first, second = summary(x, pt, range(blocks))
    t1[0] = second + half_decay * first

    pl.semaphore_wait(barrier, len(everyone))
    c_s1 = send(s1, quad_peers, 1, 0)
    c_t1 = send(t1, quad_peers, 1, 3)

    row_c, lane_c = iota((CD, CD), 0), iota((CD, CD), 1)
    perm = jnp.where(lane_c == (row_c % 8) * NG + row_c // 8, 1.0, 0.0).astype(BF16)
    flip = jnp.where(lane_c + row_c == BL - 1, 1.0, 0.0).astype(BF16)

    def regroup(k, skip_sum):
        rows = pl.ds(pl.multiple_of(k * span, span), span)
        xb, yb = x[rows, :], y[rows, :]
        for src, dst in ((xb, xg), (yb, yg)):
            turned = nt(perm, src)
            for g in range(NG):
                piece = turned[8 * g : 8 * (g + 1)]
                dst[g, pl.ds(pl.multiple_of(k * 16, 16), 16), :] = jnp.concatenate(
                    [piece[:, :BL], piece[:, BL:]], axis=0
                ).astype(BF16)
        return skip_sum + jnp.sum(xb.astype(F32) * yb.astype(F32), axis=0, keepdims=True)

    skip_sum = lax.fori_loop(0, NB // 2, regroup, jnp.zeros((1, CD), F32))

    def gram_one(g, h):
        gs = pl.ds(pl.multiple_of(g * MODES, MODES), MODES)
        xq, yq = xg[g], yg[g]
        turned = nt(flip, xq).astype(BF16)
        gram = nn(turned, yq)
        gram = pltpu.roll(gram, 1, 1, stride=1, stride_axis=0)
        lag = jnp.sum(jnp.where(lane_c <= row_c, gram, 0.0), axis=0, keepdims=True)
        powers = pw[gs, :][:, :BL]
        tails = pt[gs, :][:, BL:]
        column = jnp.sum(powers * lag, axis=1, keepdims=True)
        ph, pl_ = split(powers)
        th, tl = split(tails)
        states = nt(yq, ph) + nt(yq, pl_)
        ends = nt(xq, th) + nt(xq, tl)
        decay = jnp.exp(-(float(BL) * dec_ref[pl.ds(g, 1), :]))
        acc = jnp.zeros((8, MODES), F32)
        pieces = [acc]
        for b in range(NB - 1, 0, -1):
            acc = states[8 * b : 8 * (b + 1)] + decay * acc
            pieces.append(acc)
        held = jnp.concatenate(pieces[::-1], axis=0)
        after[g] = held
        grow[pl.ds(g, 1), 0:MODES] = jnp.sum(ends * held, axis=0, keepdims=True)
        return h + jnp.where(iota((MODES, CD), 1) == g, column, 0.0)

    def gram_some(i, h):
        for j in range(4):
            h = gram_one(i * 4 + j, h)
        return h

    h = jnp.zeros((MODES, CD), F32)
    h = lax.fori_loop(0, 2, gram_some, h)

    dev = jnp.exp(-(float(TOK) * rmc))
    quad = jnp.exp(-(float(TOK * NQ) * rmc))
    slab = jnp.exp(-(float(TOK * NQ * NZ) * rmc))
    arrive(c_s1)
    s2[0] = suffix(lambda i: s1[lax.rem(i - q + NQ, NQ)], NQ, dev)
    c_s2 = send(s2, z_peers, 1, 6)
    arrive(c_t1)
    load_s1 = lambda i: s1[lax.rem(i - q + NQ, NQ)]
    p1, tq = pairs(load_s1, lambda i: t1[lax.rem(i - q + NQ, NQ)], NQ, dev)
    t2[0] = tq
    c_t2 = send(t2, z_peers, 1, 13)

    h = lax.fori_loop(2, 4, gram_some, h)
    tmp[...] = jnp.zeros_like(tmp)
    tmp[0:NG, 0:MODES] = grow[:, 0:MODES]
    h = h + jnp.transpose(tmp[...])[:MODES]
    g1[0] = pack(h) + jnp.where(iota((8, CD), 0) == 2, skip_sum, 0.0)
    c_g1 = send(g1, quad_peers, 1, 20)

    twice = 2.0 * rates
    series = twice * (1.0 - twice / 2 * (1.0 - twice / 3 * (1.0 - twice / 4 * (
        1.0 - twice / 5 * (1.0 - twice / 6 * (1.0 - twice / 7 * (1.0 - twice / 8)))))))
    norm = jnp.sqrt(jnp.where(twice < 0.25, series, 1.0 - jnp.exp(-twice)))
    coef = res_ref[...] * norm
    tmp[...] = jnp.zeros_like(tmp)
    for k in range(CD // NG):
        tmp[NG * k : NG * (k + 1), 0:MODES] = coef
    cmc_ref[...] = jnp.transpose(tmp[...])[:MODES]

    def local_one(g):
        gs = pl.ds(pl.multiple_of(g * MODES, MODES), MODES)
        yq = yg[g]
        pick = iota((MODES, CD), 1) == g
        column = jnp.sum(jnp.where(pick, cmc_ref[...], 0.0), axis=1, keepdims=True)
        reach = column * pt[gs, :][:, BL:]
        lane = iota((MODES, BL), 1)
        taps = jnp.sum(jnp.where(lane == 0, column, reach), axis=0, keepdims=True)
        toep = pltpu.roll(jnp.broadcast_to(taps, (BL, BL)), 0, 1, stride=1, stride_axis=0)
        th, tl = split(jnp.where(lane_c <= row_c, toep, 0.0))
        ah, al = split(after[g])
        wh, wl = split(reach)
        out = nn(yq, th) + nn(yq, tl) + (nn(ah, wh) + nn(al, wh) + nn(ah, wl))
        for b in range(NB):
            ot[b, pl.ds(g, 8, stride=NG), :] = out[8 * b : 8 * (b + 1)]

    def local_some(i, _):
        for j in range(4):
            local_one(i * 4 + j)
        return _

    lax.fori_loop(0, 2, local_some, 0)
    arrive(c_g1)
    g2[0] = g1[0] + g1[1] + g1[2] + g1[3] + pack(p1)
    c_g2 = send(g2, z_peers, 1, 23)
    lax.fori_loop(2, 4, local_some, 0)

    skip_row = skip_ref[...].reshape(1, CD)

    def settle(b, _):
        rows = pl.ds(pl.multiple_of(b * BL, BL), BL)
        loc[rows, :] = jnp.transpose(ot[b]) + skip_row * y[rows, :].astype(F32)
        return _

    lax.fori_loop(0, NB, settle, 0)

    arrive(c_s2)
    load_s2 = lambda i: s2[lax.rem(i - z + NZ, NZ)]
    s3[0] = suffix(load_s2, NZ, quad)
    c_s3 = send(s3, y_peers, 1, 30)

    column = jnp.concatenate(
        [jnp.broadcast_to(rmc[:, g : g + 1], (MODES, CD)) for g in range(NG)], axis=0
    )
    rowr[...] = jnp.transpose(column)[0:8]
    hl = TOK // 2

    def reach_some(b, _):
        rows = pl.ds(pl.multiple_of(b * BL, BL), BL)
        left = (hl - b * BL - iota((BL, NG * MODES), 0)).astype(F32)
        hi, lo = split(jnp.exp(-(left * rowr[0:1, :])))
        qh[rows, :] = hi
        ql[rows, :] = lo
        return _

    lax.fori_loop(0, hl // BL, reach_some, 0)

    arrive(c_t2)
    p2, ty = pairs(load_s2, lambda i: t2[lax.rem(i - z + NZ, NZ)], NZ, quad)
    arrive(c_g2)
    gz = g2[0]
    for k in range(1, NZ):
        gz = gz + g2[k]
    m3[0, 0:16] = s3[0]
    m3[0, 16:32] = ty
    m3[0, 32:40] = gz + pack(p2)
    c_m3 = send(m3, y_peers + o_peers, 1, 33)

    arrive(c_s3)
    one = jnp.ones((MODES, CD), F32)
    zero = jnp.zeros((MODES, CD), F32)
    inc_y, w = zero, one
    for k in range(1, NY):
        inc_y = inc_y + jnp.where(yy + k < NY, w, zero) * s3[k]
        w = w * slab
    inc_z, w = zero, one
    for k in range(1, NZ):
        inc_z = inc_z + jnp.where(z + k < NZ, w, zero) * s2[k]
        w = w * quad
    inc_q, w = zero, one
    for k in range(1, NQ):
        inc_q = inc_q + jnp.where(q + k < NQ, w, zero) * s1[k]
        w = w * dev
    to_slab = jnp.exp(-(((NZ - 1 - z) * (TOK * NQ)).astype(F32) * rmc))
    to_quad = jnp.exp(-(((NQ - 1 - q) * TOK).astype(F32) * rmc))
    inc = inc_q + to_quad * (inc_z + to_slab * inc_y)

    late = cmc_ref[...] * inc
    early = late * half_decay
    group_of = iota((MODES, CD), 1) % NG

    def spread(v):
        return jnp.concatenate([jnp.where(group_of == g, v, 0.0) for g in range(NG)], axis=0)

    def both(v, u):
        return jnp.concatenate([spread(v), spread(u)], axis=1).astype(BF16)

    eh = early.astype(BF16).astype(F32)
    lh = late.astype(BF16).astype(F32)
    a_hi = both(eh, lh)
    a_lo = both(early - eh, late - lh)

    def finish(b, _):
        rows = pl.ds(pl.multiple_of(b * BL, BL), BL)
        rows2 = pl.ds(pl.multiple_of(hl + b * BL, BL), BL)
        hi, lo = qh[rows, :], ql[rows, :]
        add = nn(hi, a_hi) + nn(hi, a_lo) + nn(lo, a_hi)
        outb[rows, :] = (loc[rows, :] + add[:, :CD]).astype(BF16)
        outb[rows2, :] = (loc[rows2, :] + add[:, CD:]).astype(BF16)
        return _

    lax.fori_loop(0, hl // BL, finish, 0)
    store = pltpu.make_async_copy(outb, dx_hbm, out_sem.at[0])
    store.start()

    arrive(c_m3)

    def load_y3(lo, base):
        return lambda i: m3[base + lax.rem(i - yy + NY, NY), lo : lo + 16]

    p3, _ = pairs(load_y3(0, 0), load_y3(16, 0), NY, slab)
    p4, _ = pairs(load_y3(0, 4), load_y3(16, 4), NY, slab)
    own = m3[0, 32:40] + m3[1, 32:40] + m3[2, 32:40] + m3[3, 32:40]
    other = m3[4, 32:40] + m3[5, 32:40] + m3[6, 32:40] + m3[7, 32:40]
    total_len = TOK * NQ * NZ * NY
    sg_ref[...] = (own[2:3] * (1.0 / math.sqrt(total_len))).reshape(CD)
    grads = fold(unpack(own + other) + p3 + p4)
    tmp[...] = jnp.zeros_like(tmp)
    tmp[0:MODES, :] = grads
    turned = jnp.transpose(tmp[...])[0:NG, 0:MODES]
    rg_ref[...] = turned * norm * (1.0 / math.sqrt(GROUP * total_len))

    for copy in sent:
        copy.wait_send()
    store.wait()


def shards(inputs, cotangent, residues, decay_rates, skip_weight):
    vmem = pl.BlockSpec(memory_space=pltpu.VMEM)
    hbm = pl.BlockSpec(memory_space=pl.ANY)
    return pl.pallas_call(
        kernel,
        out_shape=(
            jax.ShapeDtypeStruct((TOK, CD), BF16),
            jax.ShapeDtypeStruct((NG, MODES), F32),
            jax.ShapeDtypeStruct((CD,), F32),
        ),
        in_specs=[hbm, hbm, vmem, vmem, vmem],
        out_specs=(hbm, vmem, vmem),
        scratch_shapes=[
            pltpu.VMEM((TOK, CD), BF16),
            pltpu.VMEM((TOK, CD), BF16),
            pltpu.VMEM((NG, CD, BL), BF16),
            pltpu.VMEM((NG, CD, BL), BF16),
            pltpu.VMEM((CD, CD), F32),
            pltpu.VMEM((MODES, CD), F32),
            pltpu.VMEM((MODES, CD), F32),
            pltpu.VMEM((NG * MODES, 2 * BL), F32),
            pltpu.VMEM((NG * MODES, 2 * BL), F32),
            pltpu.VMEM((NG, CD, MODES), F32),
            pltpu.VMEM((NG, CD), F32),
            pltpu.VMEM((NB, CD, BL), F32),
            pltpu.VMEM((TOK, CD), F32),
            pltpu.VMEM((TOK // 2, NG * MODES), BF16),
            pltpu.VMEM((TOK // 2, NG * MODES), BF16),
            pltpu.VMEM((TOK, CD), BF16),
            pltpu.VMEM((8, NG * MODES), F32),
            pltpu.VMEM((NQ, MODES, CD), F32),
            pltpu.VMEM((NQ, MODES, CD), F32),
            pltpu.VMEM((NQ, 8, CD), F32),
            pltpu.VMEM((NZ, MODES, CD), F32),
            pltpu.VMEM((NZ, MODES, CD), F32),
            pltpu.VMEM((NZ, 8, CD), F32),
            pltpu.VMEM((NY, MODES, CD), F32),
            pltpu.VMEM((2 * NY, 40, CD), F32),
            pltpu.SemaphoreType.DMA((2,)),
            pltpu.SemaphoreType.DMA((1,)),
            pltpu.SemaphoreType.DMA((40,)),
            pltpu.SemaphoreType.DMA((40,)),
        ],
        compiler_params=pltpu.CompilerParams(
            collective_id=0, has_side_effects=True, vmem_limit_bytes=32 << 20
        ),
    )(inputs, cotangent, residues, decay_rates, skip_weight)


def solution(mesh):
    placed = (P("seq", "chan"), P("seq", "chan"), P(), P(), P("chan"))
    return jax.shard_map(
        shards,
        mesh=mesh,
        in_specs=placed,
        out_specs=(P("seq", "chan"), P(), P("chan")),
        check_vma=False,
    )
```

time: 408 us -> 36.1 us (0.09)
  the two profiles are of different devices: /device:TPU:4 before, /device:TPU:1 now
where the time goes in v1:
time: 36.1 us; the launch traced here: 35.8 us
  Pallas kernels  29.1 us (81%)
  local copies, waits for them, and re-layouts  6.03 us (17%)
  between operations  0.65 us (2%)
    pallas_call x1, Pallas kernels, shards(): pl.pallas_call(kernel, out_shape=(jax.ShapeDtypeStruct((TOK, CD), BF16),...  29.1 us
    unnamed x13, local copies, waits for them, and re-layouts  6.03 us

profile of v1, /device:TPU:1, one launch (start us, length us, event | category | flops | bytes accessed | tf_op | source)
XLA Modules:
  0.0 35.8 jit_solution(6697699930014397464)
XLA Ops:
  0.6 0.0 copy-start
  0.6 1.0 %copy-done = bf16[2048,128]{1,0:T(8,128)(2,1)S(1)} copy-done((bf16[2048,128]{1,0:T(8,128)(2,1)S(1)}, bf16[2048,128]{1,0:T(8,128)(2,1)}, u32[]{:S(2)}) %copy-start) | copy-done | bytes 524312
  1.7 0.0 copy-start.1
  1.7 1.0 %copy-done.1 = bf16[2048,128]{1,0:T(8,128)(2,1)S(1)} copy-done((bf16[2048,128]{1,0:T(8,128)(2,1)S(1)}, bf16[2048,128]{1,0:T(8,128)(2,1)}, u32[]{:S(2)}) %copy-start.1) | copy-done | bytes 524312
  2.7 0.0 copy-start.2
  2.7 0.7 %copy-done.2 = f32[16,16]{1,0:T(8,128)S(1)} copy-done((f32[16,16]{1,0:T(8,128)S(1)}, f32[16,16]{1,0:T(8,128)}, u32[]{:S(2)}) %copy-start.2) | copy-done | bytes 1048
  3.4 0.0 copy-start.3
  3.4 0.7 %copy-done.3 = f32[16,16]{1,0:T(8,128)S(1)} copy-done((f32[16,16]{1,0:T(8,128)S(1)}, f32[16,16]{1,0:T(8,128)}, u32[]{:S(2)}) %copy-start.3) | copy-done | bytes 1048
  4.1 0.0 copy-start.4
  4.1 0.7 %copy-done.4 = f32[128]{0:T(128)S(1)} copy-done((f32[128]{0:T(128)S(1)}, f32[128]{0:T(128)}, u32[]{:S(2)}) %copy-start.4) | copy-done | bytes 536
  4.8 29.1 %shard_map.76 = (bf16[2048,128]{1,0:T(8,128)(2,1)S(1)}, f32[16,16]{1,0:T(8,128)S(1)}, f32[128]{0:T(128)S(1)}) custom-call(bf16[2048,128]{1,0:T(8,128)(2,1)S(1)} %copy-done, bf16[2048,128]{1,0:T(8,128)(2,1)S(1)} %copy-done.1, f32[16,16]{1,0:T(8,128)S(1)} %copy-done.2, f32[16,16]{1,0:T(8,128)S(1)} %copy-done.3, f32[128]{0:T(128)S(1)} %copy-done.4), custom_call_target="tpu_custom_call" | custom-call | tf_op jit(solution)/shard_map/pallas_call | solution.py:402
  33.9 0.8 %copy.11 = bf16[2048,128]{1,0:T(8,128)(2,1)} copy(bf16[2048,128]{1,0:T(8,128)(2,1)S(1)} %get-tuple-element.6) | data formatting | bytes 1048576
  34.7 0.6 %copy.12 = f32[16,16]{1,0:T(8,128)} copy(f32[16,16]{1,0:T(8,128)S(1)} %get-tuple-element.7) | data formatting | bytes 2048
  35.3 0.5 %copy.13 = f32[128]{0:T(128)} copy(f32[128]{0:T(128)S(1)} %get-tuple-element.8) | data formatting | bytes 1024
Async XLA Ops:
  0.6 1.0 %copy-start = (bf16[2048,128]{1,0:T(8,128)(2,1)S(1)}, bf16[2048,128]{1,0:T(8,128)(2,1)}, u32[]{:S(2)}) copy-start(bf16[2048,128]{1,0:T(8,128)(2,1)} %x_hbm.1) | copy-start | bytes 1572868
  1.7 1.0 %copy-start.1 = (bf16[2048,128]{1,0:T(8,128)(2,1)S(1)}, bf16[2048,128]{1,0:T(8,128)(2,1)}, u32[]{:S(2)}) copy-start(bf16[2048,128]{1,0:T(8,128)(2,1)} %y_hbm.1) | copy-start | bytes 1572868
  2.7 0.7 %copy-start.2 = (f32[16,16]{1,0:T(8,128)S(1)}, f32[16,16]{1,0:T(8,128)}, u32[]{:S(2)}) copy-start(f32[16,16]{1,0:T(8,128)} %res_ref.1) | copy-start | bytes 3076
  3.4 0.7 %copy-start.3 = (f32[16,16]{1,0:T(8,128)S(1)}, f32[16,16]{1,0:T(8,128)}, u32[]{:S(2)}) copy-start(f32[16,16]{1,0:T(8,128)} %dec_ref.1) | copy-start | bytes 3076
  4.1 0.7 %copy-start.4 = (f32[128]{0:T(128)S(1)}, f32[128]{0:T(128)}, u32[]{:S(2)}) copy-start(f32[128]{0:T(128)} %skip_ref.1) | copy-start | bytes 1540

commit v2 on v1

--- a/solution.py
+++ b/solution.py
@@ -85,11 +85,11 @@
 
 
 def kernel(
-    x_hbm, y_hbm, res_ref, dec_ref, skip_ref,
-    dx_hbm, rg_ref, sg_ref,
-    x, y, xg, yg, tmp, rmc_ref, cmc_ref, pw, pt, after, grow, ot, loc, qh, ql, outb, rowr,
+    x_hbm, y_hbm, res_hbm, dec_hbm, skip_hbm,
+    outb, rg_ref, sg_ref,
+    x, y, res_ref, dec_ref, skip_ref, xg, yg, tmp, rmc_ref, cmc_ref, pw, pt, after, grow, ot, loc, qh, ql, rowr,
     s1, t1, g1, s2, t2, g2, s3, m3,
-    load_sem, out_sem, send_sem, recv_sem,
+    load_sem, send_sem, recv_sem,
 ):
     me = lax.axis_index("seq")
     half = lax.axis_index("chan")
@@ -107,8 +107,11 @@
 
     load_y = pltpu.make_async_copy(y_hbm, y, load_sem.at[0])
     load_x = pltpu.make_async_copy(x_hbm, x, load_sem.at[1])
-    load_y.start()
-    load_x.start()
+    load_r = pltpu.make_async_copy(res_hbm, res_ref, load_sem.at[2])
+    load_d = pltpu.make_async_copy(dec_hbm, dec_ref, load_sem.at[3])
+    load_k = pltpu.make_async_copy(skip_hbm, skip_ref, load_sem.at[4])
+    for copy in (load_d, load_y, load_x, load_r, load_k):
+        copy.start()
     barrier = pltpu.get_barrier_semaphore()
     everyone = quad_peers + z_peers + y_peers + o_peers
     for peer in everyone:
@@ -137,6 +140,7 @@
         for copy in copies:
             copy.wait_recv()
 
+    load_d.wait()
     rates = dec_ref[...]
     tmp[...] = jnp.zeros_like(tmp)
     for k in range(CD // NG):
@@ -172,6 +176,8 @@
     first, second = summary(y, pw, range(blocks - 1, -1, -1))
     s1[0] = first + half_decay * second
     load_x.wait()
+    load_r.wait()
+    load_k.wait()
     first, second = summary(x, pt, range(blocks))
     t1[0] = second + half_decay * first
 
@@ -371,8 +377,6 @@
         return _
 
     lax.fori_loop(0, hl // BL, finish, 0)
-    store = pltpu.make_async_copy(outb, dx_hbm, out_sem.at[0])
-    store.start()
 
     arrive(c_m3)
 
@@ -393,24 +397,37 @@
 
     for copy in sent:
         copy.wait_send()
-    store.wait()
+
+
+def deliver(a, b, c, to_a, to_b, to_c, sems):
+    copies = [
+        pltpu.make_async_copy(src, dst, sems.at[i])
+        for i, (src, dst) in enumerate(((a, to_a), (b, to_b), (c, to_c)))
+    ]
+    for copy in copies:
+        copy.start()
+    for copy in copies:
+        copy.wait()
 
 
 def shards(inputs, cotangent, residues, decay_rates, skip_weight):
     vmem = pl.BlockSpec(memory_space=pltpu.VMEM)
-    hbm = pl.BlockSpec(memory_space=pl.ANY)
-    return pl.pallas_call(
+    hbm = pl.BlockSpec(memory_space=pltpu.HBM)
+    near = pl.pallas_call(
         kernel,
         out_shape=(
-            jax.ShapeDtypeStruct((TOK, CD), BF16),
-            jax.ShapeDtypeStruct((NG, MODES), F32),
-            jax.ShapeDtypeStruct((CD,), F32),
+            pltpu.VMEM((TOK, CD), BF16),
+            pltpu.VMEM((NG, MODES), F32),
+            pltpu.VMEM((CD,), F32),
         ),
-        in_specs=[hbm, hbm, vmem, vmem, vmem],
-        out_specs=(hbm, vmem, vmem),
+        in_specs=[hbm] * 5,
+        out_specs=(vmem, vmem, vmem),
         scratch_shapes=[
             pltpu.VMEM((TOK, CD), BF16),
             pltpu.VMEM((TOK, CD), BF16),
+            pltpu.VMEM((NG, MODES), F32),
+            pltpu.VMEM((NG, MODES), F32),
+            pltpu.VMEM((CD,), F32),
             pltpu.VMEM((NG, CD, BL), BF16),
             pltpu.VMEM((NG, CD, BL), BF16),
             pltpu.VMEM((CD, CD), F32),
@@ -424,7 +441,6 @@
             pltpu.VMEM((TOK, CD), F32),
             pltpu.VMEM((TOK // 2, NG * MODES), BF16),
             pltpu.VMEM((TOK // 2, NG * MODES), BF16),
-            pltpu.VMEM((TOK, CD), BF16),
             pltpu.VMEM((8, NG * MODES), F32),
             pltpu.VMEM((NQ, MODES, CD), F32),
             pltpu.VMEM((NQ, MODES, CD), F32),
@@ -434,15 +450,25 @@
             pltpu.VMEM((NZ, 8, CD), F32),
             pltpu.VMEM((NY, MODES, CD), F32),
             pltpu.VMEM((2 * NY, 40, CD), F32),
-            pltpu.SemaphoreType.DMA((2,)),
-            pltpu.SemaphoreType.DMA((1,)),
+            pltpu.SemaphoreType.DMA((5,)),
             pltpu.SemaphoreType.DMA((40,)),
             pltpu.SemaphoreType.DMA((40,)),
         ],
         compiler_params=pltpu.CompilerParams(
             collective_id=0, has_side_effects=True, vmem_limit_bytes=32 << 20
         ),
-    )(inputs, cotangent, residues, decay_rates, skip_weight)
+    )(*[pltpu.with_memory_space_constraint(v, pltpu.HBM) for v in (inputs, cotangent, residues, decay_rates, skip_weight)])
+    return pl.pallas_call(
+        deliver,
+        out_shape=(
+            jax.ShapeDtypeStruct((TOK, CD), BF16),
+            jax.ShapeDtypeStruct((NG, MODES), F32),
+            jax.ShapeDtypeStruct((CD,), F32),
+        ),
+        in_specs=[vmem, vmem, vmem],
+        out_specs=(hbm, hbm, hbm),
+        scratch_shapes=[pltpu.SemaphoreType.DMA((3,))],
+    )(*[pltpu.with_memory_space_constraint(v, pltpu.VMEM) for v in near])
 
 
 def solution(mesh):

time: 36.1 us -> 30.7 us (0.85)
  local copies, waits for them, and re-layouts: 6.03 us -> 0 us
  Pallas kernels: 29.1 us -> 29.9 us
    unnamed x13 -> x0, local copies, waits for them, and re-layouts: 6.03 us -> none
    pallas_call x1 -> x2, Pallas kernels: 29.1 us -> 29.9 us  [the longest x1 29.1 us: shards(): pl.pallas_call(kernel, out_shape=(pltpu.VMEM((TOK, CD), BF16), pltpu.VMEM...]
where the time goes in v2:
time: 30.7 us; the launch traced here: 30.6 us
  Pallas kernels  29.9 us (97%)
  between operations  0.64 us (2%)
    pallas_call x1, Pallas kernels, shards(): pl.pallas_call(kernel, out_shape=(pltpu.VMEM((TOK, CD), BF16), pltpu.VMEM...  29.1 us
    pallas_call x1, Pallas kernels, shards(): pl.pallas_call(deliver, out_shape=(jax.ShapeDtypeStruct((TOK, CD), BF16),...  0.83 us

profile of v2, /device:TPU:1, one launch (start us, length us, event | category | flops | bytes accessed | tf_op | source)
XLA Modules:
  0.0 30.6 jit_solution(16985063685762258162)
XLA Ops:
  0.6 29.1 %shard_map.76 = (bf16[2048,128]{1,0:T(8,128)(2,1)S(1)}, f32[16,16]{1,0:T(8,128)S(1)}, f32[128]{0:T(128)S(1)}) custom-call(bf16[2048,128]{1,0:T(8,128)(2,1)} %x_hbm.1, bf16[2048,128]{1,0:T(8,128)(2,1)} %y_hbm.1, f32[16,16]{1,0:T(8,128)} %res_hbm.1, f32[16,16]{1,0:T(8,128)} %dec_hbm.1, f32[128]{0:T(128)} %skip_hbm.1), custom_call_target="tpu_custom_call" | custom-call | tf_op jit(solution)/shard_map/pallas_call | solution.py:416
  29.7 0.8 %shard_map.77 = (bf16[2048,128]{1,0:T(8,128)(2,1)}, f32[16,16]{1,0:T(8,128)}, f32[128]{0:T(128)}) custom-call(bf16[2048,128]{1,0:T(8,128)(2,1)S(1)} %get-tuple-element.6.a, f32[16,16]{1,0:T(8,128)S(1)} %get-tuple-element.7.b, f32[128]{0:T(128)S(1)} %get-tuple-element.8.c), custom_call_target="tpu_custom_call" | custom-call | tf_op jit(solution)/shard_map/pallas_call | solution.py:461

commit v3 on v2

v3 whole, which is shorter than its diff:
```python
import math

import jax
import jax.numpy as jnp
from jax import lax
from jax.experimental import pallas as pl
from jax.experimental.pallas import tpu as pltpu
from jax.sharding import PartitionSpec as P

MESH = pl.DeviceIdType.MESH
F32 = jnp.float32
BF16 = jnp.bfloat16
NG = 16
MODES = 16
GROUP = 16
TOK = 2048
CD = 128
BL = 128
NB = TOK // BL
NQ, NZ, NY = 4, 8, 4


def split(v):
    hi = v.astype(BF16)
    return hi, (v - hi.astype(F32)).astype(BF16)


def nn(a, b):
    return lax.dot_general(a, b, (((1,), (0,)), ((), ())), preferred_element_type=F32)


def nt(a, b):
    return lax.dot_general(a, b, (((1,), (1,)), ((), ())), preferred_element_type=F32)


def iota(shape, dim):
    return lax.broadcasted_iota(jnp.int32, shape, dim)


def fold(h):
    h = h + pltpu.roll(h, 64, 1)
    h = h + pltpu.roll(h, 32, 1)
    return h + pltpu.roll(h, 16, 1)


def pack(h):
    h = fold(h)
    keep = iota((8, CD), 1) // 16 == iota((8, CD), 0)
    first = jnp.sum(jnp.where(keep, h[:8], 0.0), axis=0, keepdims=True)
    second = jnp.sum(jnp.where(keep, h[8:], 0.0), axis=0, keepdims=True)
    row = iota((8, CD), 0)
    return jnp.where(row == 0, first, jnp.where(row == 1, second, 0.0))


def unpack(tile):
    keep = iota((8, CD), 1) // 16 == iota((8, CD), 0)
    return jnp.concatenate(
        [jnp.where(keep, tile[0:1], 0.0), jnp.where(keep, tile[1:2], 0.0)], axis=0
    )


def extract(full):
    group_of = iota((MODES, CD), 1) % NG
    out = jnp.zeros((MODES, CD), F32)
    for g in range(NG):
        out = out + jnp.where(group_of == g, full[MODES * g : MODES * (g + 1)], 0.0)
    return out


def suffix(load_s, count, w):
    acc = load_s(count - 1)
    for i in range(count - 2, -1, -1):
        acc = load_s(i) + w * acc
    return acc


def pairs(load_s, load_t, count, w):
    acc = load_t(0)
    total = None
    for i in range(1, count):
        term = acc * load_s(i)
        total = term if total is None else total + term
        acc = load_t(i) + w * acc
    return total, acc


def exchange(blocks):
    bit_of = iota(blocks[0].shape, 1)
    for k in (1, 2, 4, 8):
        keep = (bit_of & k) == 0
        for i in range(NG):
            if not i & k:
                low, high = blocks[i], blocks[i | k]
                blocks[i] = jnp.where(keep, low, pltpu.roll(high, k, 1))
                blocks[i | k] = jnp.where(keep, pltpu.roll(low, CD - k, 1), high)
    return blocks


def kernel(
    x_hbm, y_hbm, res_hbm, dec_hbm, skip_hbm,
    outb, rg_ref, sg_ref,
    x, y, res_ref, dec_ref, skip_ref, xn, yn, tmp, cmc_ref, rates3, pw, pt, zs, tb, lags, after, on, loc, qh, ql,
    s1, t1, s2, t2, s3, m3, gz, gy, gq,
    load_sem, send_sem, recv_sem,
):
    me = lax.axis_index("seq")
    half = lax.axis_index("chan")
    q = lax.rem(me, NQ)
    z = lax.rem(me // NQ, NZ)
    yy = me // (NQ * NZ)

    def at(y_i, z_i, q_i, h_i):
        return {"seq": (y_i * NZ + z_i) * NQ + q_i, "chan": h_i}

    quad_peers = [(k, at(yy, z, lax.rem(q + NQ - k, NQ), half)) for k in (2, 3, 1)]
    z_peers = [(k, at(yy, lax.rem(z + NZ - k, NZ), q, half)) for k in (4, 3, 5, 2, 6, 1, 7)]
    y_peers = [(k, at(lax.rem(yy + NY - k, NY), z, q, half)) for k in (2, 1, 3)]
    o_peers = [(NY + k, at(lax.rem(yy + NY - k, NY), z, q, 1 - half)) for k in (2, 1, 3, 0)]

    load_y = pltpu.make_async_copy(y_hbm, y, load_sem.at[0])
    load_x = pltpu.make_async_copy(x_hbm, x, load_sem.at[1])
    load_r = pltpu.make_async_copy(res_hbm, res_ref, load_sem.at[2])
    load_d = pltpu.make_async_copy(dec_hbm, dec_ref, load_sem.at[3])
    load_k = pltpu.make_async_copy(skip_hbm, skip_ref, load_sem.at[4])
    load_d.start()
    load_y.start()
    barrier = pltpu.get_barrier_semaphore()
    everyone = z_peers + o_peers + y_peers + quad_peers
    for _, peer in everyone:
        pl.semaphore_signal(barrier, inc=1, device_id=peer, device_id_type=MESH)
    load_x.start()
    load_r.start()
    load_k.start()

    sent = []

    def send(buf, peers, sem):
        copies = []
        for slot, peer in peers:
            copy = pltpu.make_async_remote_copy(
                src_ref=buf.at[0],
                dst_ref=buf.at[slot],
                send_sem=send_sem.at[sem + slot],
                recv_sem=recv_sem.at[sem + slot],
                device_id=peer,
                device_id_type=MESH,
            )
            copy.start()
            copies.append(copy)
        sent.extend(copies)
        return copies

    def arrive(copies):
        for copy in copies:
            copy.wait_recv()

    load_d.wait()
    rates = dec_ref[...]
    tmp[...] = jnp.zeros_like(tmp)
    for k in range(CD // NG):
        tmp[NG * k : NG * (k + 1), 0:MODES] = rates
    rmc = jnp.transpose(tmp[...])[:MODES]
    for k in range(3):
        rates3[:, MODES * k : MODES * (k + 1)] = rates
    span = 2 * BL
    ahead = iota((MODES, span), 1).astype(F32)
    behind = span - ahead
    for g in range(NG):
        column = jnp.broadcast_to(rmc[:, g : g + 1], (MODES, span))
        pw[MODES * g : MODES * (g + 1), :] = jnp.exp(-(column * ahead))
        pt[MODES * g : MODES * (g + 1), :] = jnp.exp(-(column * behind))

    wide = jnp.broadcast_to(pt[:, 0:1], (NG * MODES, 2 * CD))
    half_decay = jnp.exp(-(float(TOK // 2) * rmc))
    blocks = TOK // 2 // span

    def summary(ref, powers, order):
        hi, lo = split(powers[...])
        total = None
        for b in order:
            both = jnp.concatenate(
                [ref[b * span : (b + 1) * span, :], ref[TOK // 2 + b * span : TOK // 2 + (b + 1) * span, :]],
                axis=1,
            )
            part = nn(hi, both) + nn(lo, both)
            total = part if total is None else part + wide * total
        return extract(total[:, :CD]), extract(total[:, CD:])

    load_y.wait()
    first, second = summary(y, pw, range(blocks - 1, -1, -1))
    s1[0] = first + half_decay * second
    load_x.wait()
    load_r.wait()
    load_k.wait()
    first, second = summary(x, pt, range(blocks))
    t1[0] = second + half_decay * first

    def regroup(src, dst, step):
        for r in range(0, BL, step):
            for g, piece in enumerate(exchange([src[b * BL + r : b * BL + r + step, :] for b in range(NB)])):
                dst[g, r : r + step, :] = piece

    regroup(y, yn, 32)
    regroup(x, xn, 32)

    pl.semaphore_wait(barrier, len(everyone))
    c_s1 = send(s1, quad_peers, 0)
    c_t1 = send(t1, quad_peers, 4)

    row_c, lane_c = iota((BL, BL), 0), iota((BL, BL), 1)
    flip = jnp.where(lane_c + row_c == BL - 1, 1.0, 0.0).astype(BF16)
    for g in range(NG):
        gs = slice(MODES * g, MODES * (g + 1))
        ph, pl_ = split(pw[gs, :BL])
        th, tl = split(pt[gs, BL:])
        yq, xq = yn[g], xn[g]
        part = nn(jnp.concatenate([ph, pl_], axis=0), yq)
        zs[gs, :] = part[:MODES] + part[MODES:]
        part = nn(jnp.concatenate([flip, th, tl], axis=0), xq)
        tb[gs, :] = part[BL : BL + MODES] + part[BL + MODES :]
        gram = nt(part[:BL].astype(BF16), yq)
        gram = pltpu.roll(gram, 1, 1, stride=1, stride_axis=0)
        lags[g : g + 1, :] = jnp.sum(jnp.where(lane_c <= row_c, gram, 0.0), axis=0, keepdims=True)

    block_of = iota((NG * MODES, CD), 1) % NB
    run = zs[...]
    decay = jnp.broadcast_to(pw[:, BL : BL + 1], (NG * MODES, CD))
    for k in (1, 2, 4, 8):
        run = run + jnp.where(block_of + k < NB, decay * pltpu.roll(run, CD - k, 1), 0.0)
        decay = decay * decay
    run = jnp.where(block_of + 1 < NB, pltpu.roll(run, CD - 1, 1), 0.0)
    after[...] = run
    h = jnp.zeros((MODES, CD), F32)
    for g in range(NG):
        gs = slice(MODES * g, MODES * (g + 1))
        terms = pw[gs, :BL] * lags[g : g + 1, :] + tb[gs, :] * after[gs, :]
        column = jnp.sum(terms, axis=1, keepdims=True)
        h = h + jnp.where(iota((MODES, CD), 1) == g, column, 0.0)
    skip_sum = jnp.zeros((BL, CD), F32)
    for b in range(NB):
        rows = slice(b * BL, (b + 1) * BL)
        skip_sum = skip_sum + x[rows, :].astype(F32) * y[rows, :].astype(F32)
    skip_sum = jnp.sum(skip_sum, axis=0, keepdims=True)
    gz[0] = pack(h) + jnp.where(iota((8, CD), 0) == 2, skip_sum, 0.0)
    c_gz = send(gz, z_peers, 8)

    dev = jnp.exp(-(float(TOK) * rmc))
    quad = jnp.exp(-(float(TOK * NQ) * rmc))
    slab = jnp.exp(-(float(TOK * NQ * NZ) * rmc))
    load_s1 = lambda i: s1[lax.rem(i - q + NQ, NQ)]
    arrive(c_s1)
    s2[0] = suffix(load_s1, NQ, dev)
    c_s2 = send(s2, z_peers, 16)
    arrive(c_t1)
    p1, tq = pairs(load_s1, lambda i: t1[lax.rem(i - q + NQ, NQ)], NQ, dev)
    t2[0, 0:16] = tq
    t2[0, 16:24] = pack(p1)
    c_t2 = send(t2, z_peers, 24)

    twice = 2.0 * rates
    series = twice * (1.0 - twice / 2 * (1.0 - twice / 3 * (1.0 - twice / 4 * (
        1.0 - twice / 5 * (1.0 - twice / 6 * (1.0 - twice / 7 * (1.0 - twice / 8)))))))
    norm = jnp.sqrt(jnp.where(twice < 0.25, series, 1.0 - jnp.exp(-twice)))
    coef = res_ref[...] * norm
    for k in range(CD // NG):
        tmp[NG * k : NG * (k + 1), 0:MODES] = coef
    cmc_ref[...] = jnp.transpose(tmp[...])[:MODES]

    third = iota((BL, 3 * MODES), 1) // MODES
    left = (BL - iota((BL, 3 * MODES), 0)).astype(F32)

    def local_one(g):
        gs = slice(MODES * g, MODES * (g + 1))
        yq = yn[g]
        column = jnp.broadcast_to(cmc_ref[:, g : g + 1], (MODES, CD))
        taps = jnp.sum(column * pw[gs, :BL], axis=0, keepdims=True)
        toep = pltpu.roll(jnp.broadcast_to(taps, (BL, BL)), 0, 1, stride=1, stride_axis=0)
        th, tl = split(jnp.where(lane_c >= row_c, toep, 0.0))
        ah, al = split(column * after[gs, :])
        reach = jnp.exp(-(left * rates3[g : g + 1, :]))
        rh = reach.astype(BF16).astype(F32)
        reach = jnp.where(third == 1, reach - rh, rh).astype(BF16)
        on[g] = nn(
            jnp.concatenate([th, tl], axis=1), jnp.concatenate([yq, yq], axis=0)
        ) + nn(reach, jnp.concatenate([ah, ah, al], axis=0))

    for g in range(NG):
        local_one(g)

    skip_row = skip_ref[...].reshape(1, CD)
    for r in range(0, BL, 16):
        for b, piece in enumerate(exchange([on[g, r : r + 16, :] for g in range(NG)])):
            rows = slice(b * BL + r, b * BL + r + 16)
            loc[rows, :] = piece + skip_row * y[rows, :].astype(F32)

    def add_up(buf, count):
        total = buf[0]
        for k in range(1, count):
            total = total + buf[k]
        return total

    own_row = iota((8, CD), 0) == 2
    arrive(c_gz)
    gy[0] = add_up(gz, NZ)
    c_gy = send(gy, y_peers + o_peers, 32)

    hl = TOK // 2
    column = jnp.concatenate(
        [jnp.broadcast_to(rmc[:, g : g + 1], (MODES, CD)) for g in range(NG)], axis=0
    )
    rowr = jnp.transpose(column)[0:1]
    for b in range(hl // BL):
        rows = slice(b * BL, (b + 1) * BL)
        away = (hl - b * BL - iota((BL, NG * MODES), 0)).astype(F32)
        qh[rows, :], ql[rows, :] = split(jnp.exp(-(away * rowr)))

    arrive(c_s2)
    load_s2 = lambda i: s2[lax.rem(i - z + NZ, NZ)]
    s3[0] = suffix(load_s2, NZ, quad)
    c_s3 = send(s3, y_peers, 40)
    arrive(c_t2)
    p2, ty = pairs(load_s2, lambda i: t2[lax.rem(i - z + NZ, NZ), 0:16], NZ, quad)
    g2 = pack(p2)
    for k in range(NZ):
        g2 = g2 + t2[k, 16:24]
    m3[0, 0:16] = s3[0]
    m3[0, 16:32] = ty
    m3[0, 32:40] = g2
    c_m3 = send(m3, y_peers + o_peers, 44)

    arrive(c_gy)
    both_halves = add_up(gy, 2 * NY)
    own_half = gy[0] + gy[1] + gy[2] + gy[3]
    gq[0] = jnp.where(own_row, own_half, both_halves)
    c_gq = send(gq, quad_peers, 52)

    arrive(c_s3)
    one = jnp.ones((MODES, CD), F32)
    zero = jnp.zeros((MODES, CD), F32)
    inc_y, w = zero, one
    for k in range(1, NY):
        inc_y = inc_y + jnp.where(yy + k < NY, w, zero) * s3[k]
        w = w * slab
    inc_z, w = zero, one
    for k in range(1, NZ):
        inc_z = inc_z + jnp.where(z + k < NZ, w, zero) * s2[k]
        w = w * quad
    inc_q, w = zero, one
    for k in range(1, NQ):
        inc_q = inc_q + jnp.where(q + k < NQ, w, zero) * s1[k]
        w = w * dev
    to_slab = jnp.exp(-(((NZ - 1 - z) * (TOK * NQ)).astype(F32) * rmc))
    to_quad = jnp.exp(-(((NQ - 1 - q) * TOK).astype(F32) * rmc))
    inc = inc_q + to_quad * (inc_z + to_slab * inc_y)

    late = cmc_ref[...] * inc
    early = late * half_decay
    group_of = iota((MODES, CD), 1) % NG

    def spread(v):
        return jnp.concatenate([jnp.where(group_of == g, v, 0.0) for g in range(NG)], axis=0)

    def both(v, u):
        return jnp.concatenate([spread(v), spread(u)], axis=1).astype(BF16)

    eh = early.astype(BF16).astype(F32)
    lh = late.astype(BF16).astype(F32)
    a_hi = both(eh, lh)
    a_lo = both(early - eh, late - lh)
    arrived = jnp.concatenate([a_hi, a_lo, a_hi], axis=0)
    step = 2 * BL
    for r in range(0, hl, step):
        rows, rows2 = slice(r, r + step), slice(hl + r, hl + r + step)
        hi, lo = qh[rows, :], ql[rows, :]
        add = nn(jnp.concatenate([hi, hi, lo], axis=1), arrived)
        outb[rows, :] = (loc[rows, :] + add[:, :CD]).astype(BF16)
        outb[rows2, :] = (loc[rows2, :] + add[:, CD:]).astype(BF16)

    arrive(c_gq)
    base = add_up(gq, NQ)
    total_len = TOK * NQ * NZ * NY
    sg_ref[...] = (base[2:3] * (1.0 / math.sqrt(total_len))).reshape(CD)
    arrive(c_m3)

    def load_y3(lo, base):
        return lambda i: m3[base + lax.rem(i - yy + NY, NY), lo : lo + 16]

    p3, _ = pairs(load_y3(0, 0), load_y3(16, 0), NY, slab)
    p4, _ = pairs(load_y3(0, NY), load_y3(16, NY), NY, slab)
    for k in range(2 * NY):
        base = base + m3[k, 32:40]
    grads = fold(unpack(base) + p3 + p4)
    tmp[...] = jnp.zeros_like(tmp)
    tmp[0:MODES, :] = grads
    turned = jnp.transpose(tmp[...])[0:NG, 0:MODES]
    rg_ref[...] = turned * norm * (1.0 / math.sqrt(GROUP * total_len))

    for copy in sent:
        copy.wait_send()


def deliver(a, b, c, to_a, to_b, to_c, sems):
    copies = [
        pltpu.make_async_copy(src, dst, sems.at[i])
        for i, (src, dst) in enumerate(((a, to_a), (b, to_b), (c, to_c)))
    ]
    for copy in copies:
        copy.start()
    for copy in copies:
        copy.wait()


def shards(inputs, cotangent, residues, decay_rates, skip_weight):
    vmem = pl.BlockSpec(memory_space=pltpu.VMEM)
    hbm = pl.BlockSpec(memory_space=pltpu.HBM)
    near = pl.pallas_call(
        kernel,
        out_shape=(
            pltpu.VMEM((TOK, CD), BF16),
            pltpu.VMEM((NG, MODES), F32),
            pltpu.VMEM((CD,), F32),
        ),
        in_specs=[hbm] * 5,
        out_specs=(vmem, vmem, vmem),
        scratch_shapes=[
            pltpu.VMEM((TOK, CD), BF16),
            pltpu.VMEM((TOK, CD), BF16),
            pltpu.VMEM((NG, MODES), F32),
            pltpu.VMEM((NG, MODES), F32),
            pltpu.VMEM((CD,), F32),
            pltpu.VMEM((NG, BL, CD), BF16),
            pltpu.VMEM((NG, BL, CD), BF16),
            pltpu.VMEM((CD, CD), F32),
            pltpu.VMEM((MODES, CD), F32),
            pltpu.VMEM((NG, 3 * MODES), F32),
            pltpu.VMEM((NG * MODES, 2 * BL), F32),
            pltpu.VMEM((NG * MODES, 2 * BL), F32),
            pltpu.VMEM((NG * MODES, CD), F32),
            pltpu.VMEM((NG * MODES, CD), F32),
            pltpu.VMEM((NG, BL), F32),
            pltpu.VMEM((NG * MODES, CD), F32),
            pltpu.VMEM((NG, BL, CD), F32),
            pltpu.VMEM((TOK, CD), F32),
            pltpu.VMEM((TOK // 2, NG * MODES), BF16),
            pltpu.VMEM((TOK // 2, NG * MODES), BF16),
            pltpu.VMEM((NQ, MODES, CD), F32),
            pltpu.VMEM((NQ, MODES, CD), F32),
            pltpu.VMEM((NZ, MODES, CD), F32),
            pltpu.VMEM((NZ, 24, CD), F32),
            pltpu.VMEM((NY, MODES, CD), F32),
            pltpu.VMEM((2 * NY, 40, CD), F32),
            pltpu.VMEM((NZ, 8, CD), F32),
            pltpu.VMEM((2 * NY, 8, CD), F32),
            pltpu.VMEM((NQ, 8, CD), F32),
            pltpu.SemaphoreType.DMA((5,)),
            pltpu.SemaphoreType.DMA((56,)),
            pltpu.SemaphoreType.DMA((56,)),
        ],
        compiler_params=pltpu.CompilerParams(
            collective_id=0, has_side_effects=True, vmem_limit_bytes=32 << 20
        ),
    )(*[pltpu.with_memory_space_constraint(v, pltpu.HBM) for v in (inputs, cotangent, residues, decay_rates, skip_weight)])
    return pl.pallas_call(
        deliver,
        out_shape=(
            jax.ShapeDtypeStruct((TOK, CD), BF16),
            jax.ShapeDtypeStruct((NG, MODES), F32),
            jax.ShapeDtypeStruct((CD,), F32),
        ),
        in_specs=[vmem, vmem, vmem],
        out_specs=(hbm, hbm, hbm),
        scratch_shapes=[pltpu.SemaphoreType.DMA((3,))],
    )(*[pltpu.with_memory_space_constraint(v, pltpu.VMEM) for v in near])


def solution(mesh):
    placed = (P("seq", "chan"), P("seq", "chan"), P(), P(), P("chan"))
    return jax.shard_map(
        shards,
        mesh=mesh,
        in_specs=placed,
        out_specs=(P("seq", "chan"), P(), P("chan")),
        check_vma=False,
    )
```

time: 30.7 us -> 28.8 us (0.938)
  Pallas kernels: 29.9 us -> 28.1 us
    pallas_call x1, Pallas kernels: 29.1 us -> 27.2 us  [shards(): pl.pallas_call(kernel, out_shape=(pltpu.VMEM((TOK, CD), BF16), pltpu.VMEM...]
where the time goes in v3:
time: 28.8 us; the launch traced here: 28.7 us
  Pallas kernels  28.1 us (98%)
  between operations  0.64 us (2%)
    pallas_call x1, Pallas kernels, shards(): pl.pallas_call(kernel, out_shape=(pltpu.VMEM((TOK, CD), BF16), pltpu.VMEM...  27.2 us
    pallas_call x1, Pallas kernels, shards(): pl.pallas_call(deliver, out_shape=(jax.ShapeDtypeStruct((TOK, CD), BF16),...  0.83 us

profile of v3, /device:TPU:1, one launch (start us, length us, event | category | flops | bytes accessed | tf_op | source)
XLA Modules:
  0.0 28.7 jit_solution(6823651374912282285)
XLA Ops:
  0.6 27.2 %shard_map.76 = (bf16[2048,128]{1,0:T(8,128)(2,1)S(1)}, f32[16,16]{1,0:T(8,128)S(1)}, f32[128]{0:T(128)S(1)}) custom-call(bf16[2048,128]{1,0:T(8,128)(2,1)} %x_hbm.1, bf16[2048,128]{1,0:T(8,128)(2,1)} %y_hbm.1, f32[16,16]{1,0:T(8,128)} %res_hbm.1, f32[16,16]{1,0:T(8,128)} %dec_hbm.1, f32[128]{0:T(128)} %skip_hbm.1), custom_call_target="tpu_custom_call" | custom-call | tf_op jit(solution)/shard_map/pallas_call | solution.py:416
  27.9 0.8 %shard_map.77 = (bf16[2048,128]{1,0:T(8,128)(2,1)}, f32[16,16]{1,0:T(8,128)}, f32[128]{0:T(128)}) custom-call(bf16[2048,128]{1,0:T(8,128)(2,1)S(1)} %get-tuple-element.6.a, f32[16,16]{1,0:T(8,128)S(1)} %get-tuple-element.7.b, f32[128]{0:T(128)S(1)} %get-tuple-element.8.c), custom_call_target="tpu_custom_call" | custom-call | tf_op jit(solution)/shard_map/pallas_call | solution.py:463

commit v4 on v3

--- a/solution.py
+++ b/solution.py
@@ -59,12 +59,15 @@
     )
 
 
-def extract(full):
-    group_of = iota((MODES, CD), 1) % NG
-    out = jnp.zeros((MODES, CD), F32)
-    for g in range(NG):
-        out = out + jnp.where(group_of == g, full[MODES * g : MODES * (g + 1)], 0.0)
-    return out
+def gather_sum(parts):
+    bit_of = iota(parts[0].shape, 1)
+    for k in (8, 4, 2, 1):
+        keep = (bit_of & k) == 0
+        parts = [
+            jnp.where(keep, low + pltpu.roll(low, CD - k, 1), high + pltpu.roll(high, k, 1))
+            for low, high in zip(parts[:k], parts[k:])
+        ]
+    return parts[0]
 
 
 def suffix(load_s, count, w):
@@ -99,8 +102,8 @@
 def kernel(
     x_hbm, y_hbm, res_hbm, dec_hbm, skip_hbm,
     outb, rg_ref, sg_ref,
-    x, y, res_ref, dec_ref, skip_ref, xn, yn, tmp, cmc_ref, rates3, pw, pt, zs, tb, lags, after, on, loc, qh, ql,
-    s1, t1, s2, t2, s3, m3, gz, gy, gq,
+    x, y, res_ref, dec_ref, skip_ref, xn, yn, tmp, cmc_ref, rates3, pw, pt, ws, wt, zs, tb, lags, after, on, xr, loc, qh, ql,
+    m1, m2, m3, gz, gq,
     load_sem, send_sem, recv_sem,
 ):
     me = lax.axis_index("seq")
@@ -122,12 +125,12 @@
     load_r = pltpu.make_async_copy(res_hbm, res_ref, load_sem.at[2])
     load_d = pltpu.make_async_copy(dec_hbm, dec_ref, load_sem.at[3])
     load_k = pltpu.make_async_copy(skip_hbm, skip_ref, load_sem.at[4])
-    load_d.start()
-    load_y.start()
     barrier = pltpu.get_barrier_semaphore()
     everyone = z_peers + o_peers + y_peers + quad_peers
     for _, peer in everyone:
         pl.semaphore_signal(barrier, inc=1, device_id=peer, device_id_type=MESH)
+    load_d.start()
+    load_y.start()
     load_x.start()
     load_r.start()
     load_k.start()
@@ -135,24 +138,22 @@
     sent = []
 
     def send(buf, peers, sem):
-        copies = []
         for slot, peer in peers:
-            copy = pltpu.make_async_remote_copy(
+            pltpu.make_async_remote_copy(
                 src_ref=buf.at[0],
                 dst_ref=buf.at[slot],
-                send_sem=send_sem.at[sem + slot],
-                recv_sem=recv_sem.at[sem + slot],
+                send_sem=send_sem.at[sem],
+                recv_sem=recv_sem.at[sem],
                 device_id=peer,
                 device_id_type=MESH,
-            )
-            copy.start()
-            copies.append(copy)
-        sent.extend(copies)
-        return copies
+            ).start()
+        slots = [slot for slot, _ in peers]
+        area = buf.at[min(slots) : max(slots) + 1]
+        sent.append(pltpu.make_async_copy(area, area, send_sem.at[sem]))
+        return pltpu.make_async_copy(area, area, recv_sem.at[sem])
 
     def arrive(copies):
-        for copy in copies:
-            copy.wait_recv()
+        copies.wait()
 
     load_d.wait()
     rates = dec_ref[...]
@@ -165,60 +166,54 @@
     span = 2 * BL
     ahead = iota((MODES, span), 1).astype(F32)
     behind = span - ahead
+    in_block = (BL * (iota((MODES, CD), 1) % NB)).astype(F32)
+    out_block = float(BL * (NB - 1)) - in_block
     for g in range(NG):
         column = jnp.broadcast_to(rmc[:, g : g + 1], (MODES, span))
         pw[MODES * g : MODES * (g + 1), :] = jnp.exp(-(column * ahead))
         pt[MODES * g : MODES * (g + 1), :] = jnp.exp(-(column * behind))
-
-    wide = jnp.broadcast_to(pt[:, 0:1], (NG * MODES, 2 * CD))
-    half_decay = jnp.exp(-(float(TOK // 2) * rmc))
-    blocks = TOK // 2 // span
-
-    def summary(ref, powers, order):
-        hi, lo = split(powers[...])
-        total = None
-        for b in order:
-            both = jnp.concatenate(
-                [ref[b * span : (b + 1) * span, :], ref[TOK // 2 + b * span : TOK // 2 + (b + 1) * span, :]],
-                axis=1,
-            )
-            part = nn(hi, both) + nn(lo, both)
-            total = part if total is None else part + wide * total
-        return extract(total[:, :CD]), extract(total[:, CD:])
-
-    load_y.wait()
-    first, second = summary(y, pw, range(blocks - 1, -1, -1))
-    s1[0] = first + half_decay * second
-    load_x.wait()
-    load_r.wait()
-    load_k.wait()
-    first, second = summary(x, pt, range(blocks))
-    t1[0] = second + half_decay * first
+        ws[MODES * g : MODES * (g + 1), :] = jnp.exp(-(column[:, :CD] * in_block))
+        wt[MODES * g : MODES * (g + 1), :] = jnp.exp(-(column[:, :CD] * out_block))
 
     def regroup(src, dst, step):
         for r in range(0, BL, step):
             for g, piece in enumerate(exchange([src[b * BL + r : b * BL + r + step, :] for b in range(NB)])):
                 dst[g, r : r + step, :] = piece
 
-    regroup(y, yn, 32)
-    regroup(x, xn, 32)
-
-    pl.semaphore_wait(barrier, len(everyone))
-    c_s1 = send(s1, quad_peers, 0)
-    c_t1 = send(t1, quad_peers, 4)
-
     row_c, lane_c = iota((BL, BL), 0), iota((BL, BL), 1)
     flip = jnp.where(lane_c + row_c == BL - 1, 1.0, 0.0).astype(BF16)
+    half_decay = jnp.exp(-(float(TOK // 2) * rmc))
+    load_y.wait()
+    regroup(y, yn, 32)
+    parts = []
     for g in range(NG):
         gs = slice(MODES * g, MODES * (g + 1))
-        ph, pl_ = split(pw[gs, :BL])
-        th, tl = split(pt[gs, BL:])
-        yq, xq = yn[g], xn[g]
-        part = nn(jnp.concatenate([ph, pl_], axis=0), yq)
-        zs[gs, :] = part[:MODES] + part[MODES:]
-        part = nn(jnp.concatenate([flip, th, tl], axis=0), xq)
-        tb[gs, :] = part[BL : BL + MODES] + part[BL + MODES :]
-        gram = nt(part[:BL].astype(BF16), yq)
+        hi, lo = split(pw[gs, :BL])
+        part = nn(jnp.concatenate([hi, lo], axis=0), yn[g])
+        part = part[:MODES] + part[MODES:]
+        zs[gs, :] = part
+        parts.append(part * ws[gs, :])
+    m1[0, 0:16] = gather_sum(parts)
+    load_x.wait()
+    load_r.wait()
+    load_k.wait()
+    regroup(x, xn, 32)
+    parts = []
+    for g in range(NG):
+        gs = slice(MODES * g, MODES * (g + 1))
+        hi, lo = split(pt[gs, BL:])
+        part = nn(jnp.concatenate([flip, hi, lo], axis=0), xn[g])
+        xr[g] = part[:BL].astype(BF16)
+        part = part[BL : BL + MODES] + part[BL + MODES :]
+        tb[gs, :] = part
+        parts.append(part * wt[gs, :])
+    m1[0, 16:32] = gather_sum(parts)
+
+    pl.semaphore_wait(barrier, len(everyone))
+    c_m1 = send(m1, quad_peers, 0)
+
+    for g in range(NG):
+        gram = nt(xr[g], yn[g])
         gram = pltpu.roll(gram, 1, 1, stride=1, stride_axis=0)
         lags[g : g + 1, :] = jnp.sum(jnp.where(lane_c <= row_c, gram, 0.0), axis=0, keepdims=True)
 
@@ -242,20 +237,18 @@
         skip_sum = skip_sum + x[rows, :].astype(F32) * y[rows, :].astype(F32)
     skip_sum = jnp.sum(skip_sum, axis=0, keepdims=True)
     gz[0] = pack(h) + jnp.where(iota((8, CD), 0) == 2, skip_sum, 0.0)
-    c_gz = send(gz, z_peers, 8)
+    c_gz = send(gz, z_peers, 1)
 
     dev = jnp.exp(-(float(TOK) * rmc))
     quad = jnp.exp(-(float(TOK * NQ) * rmc))
     slab = jnp.exp(-(float(TOK * NQ * NZ) * rmc))
-    load_s1 = lambda i: s1[lax.rem(i - q + NQ, NQ)]
-    arrive(c_s1)
-    s2[0] = suffix(load_s1, NQ, dev)
-    c_s2 = send(s2, z_peers, 16)
-    arrive(c_t1)
-    p1, tq = pairs(load_s1, lambda i: t1[lax.rem(i - q + NQ, NQ)], NQ, dev)
-    t2[0, 0:16] = tq
-    t2[0, 16:24] = pack(p1)
-    c_t2 = send(t2, z_peers, 24)
+    arrive(c_m1)
+    load1 = lambda lo: lambda i: m1[lax.rem(i - q + NQ, NQ), lo : lo + 16]
+    m2[0, 0:16] = suffix(load1(0), NQ, dev)
+    p1, tq = pairs(load1(0), load1(16), NQ, dev)
+    m2[0, 16:32] = tq
+    m2[0, 32:40] = pack(p1)
+    c_m2 = send(m2, z_peers, 2)
 
     twice = 2.0 * rates
     series = twice * (1.0 - twice / 2 * (1.0 - twice / 3 * (1.0 - twice / 4 * (
@@ -299,10 +292,9 @@
             total = total + buf[k]
         return total
 
-    own_row = iota((8, CD), 0) == 2
     arrive(c_gz)
-    gy[0] = add_up(gz, NZ)
-    c_gy = send(gy, y_peers + o_peers, 32)
+    gq[0] = add_up(gz, NZ)
+    c_gq = send(gq, quad_peers, 3)
 
     hl = TOK // 2
     column = jnp.concatenate(
@@ -314,40 +306,34 @@
         away = (hl - b * BL - iota((BL, NG * MODES), 0)).astype(F32)
         qh[rows, :], ql[rows, :] = split(jnp.exp(-(away * rowr)))
 
-    arrive(c_s2)
-    load_s2 = lambda i: s2[lax.rem(i - z + NZ, NZ)]
-    s3[0] = suffix(load_s2, NZ, quad)
-    c_s3 = send(s3, y_peers, 40)
-    arrive(c_t2)
-    p2, ty = pairs(load_s2, lambda i: t2[lax.rem(i - z + NZ, NZ), 0:16], NZ, quad)
-    g2 = pack(p2)
+    arrive(c_gq)
+    lag_part = add_up(gq, NQ)
+    arrive(c_m2)
+    load2 = lambda lo: lambda i: m2[lax.rem(i - z + NZ, NZ), lo : lo + 16]
+    m3[0, 0:16] = suffix(load2(0), NZ, quad)
+    p2, ty = pairs(load2(0), load2(16), NZ, quad)
+    m3[0, 16:32] = ty
+    lag_part = lag_part + pack(p2)
     for k in range(NZ):
-        g2 = g2 + t2[k, 16:24]
-    m3[0, 0:16] = s3[0]
-    m3[0, 16:32] = ty
-    m3[0, 32:40] = g2
-    c_m3 = send(m3, y_peers + o_peers, 44)
-
-    arrive(c_gy)
-    both_halves = add_up(gy, 2 * NY)
-    own_half = gy[0] + gy[1] + gy[2] + gy[3]
-    gq[0] = jnp.where(own_row, own_half, both_halves)
-    c_gq = send(gq, quad_peers, 52)
-
-    arrive(c_s3)
+        lag_part = lag_part + m2[k, 32:40]
+    m3[0, 32:40] = lag_part
+    c_o3 = send(m3, o_peers, 4)
+    c_m3 = send(m3, y_peers, 5)
+
+    arrive(c_m3)
     one = jnp.ones((MODES, CD), F32)
     zero = jnp.zeros((MODES, CD), F32)
     inc_y, w = zero, one
     for k in range(1, NY):
-        inc_y = inc_y + jnp.where(yy + k < NY, w, zero) * s3[k]
+        inc_y = inc_y + jnp.where(yy + k < NY, w, zero) * m3[k, 0:16]
         w = w * slab
     inc_z, w = zero, one
     for k in range(1, NZ):
-        inc_z = inc_z + jnp.where(z + k < NZ, w, zero) * s2[k]
+        inc_z = inc_z + jnp.where(z + k < NZ, w, zero) * m2[k, 0:16]
         w = w * quad
     inc_q, w = zero, one
     for k in range(1, NQ):
-        inc_q = inc_q + jnp.where(q + k < NQ, w, zero) * s1[k]
+        inc_q = inc_q + jnp.where(q + k < NQ, w, zero) * m1[k, 0:16]
         w = w * dev
     to_slab = jnp.exp(-(((NZ - 1 - z) * (TOK * NQ)).astype(F32) * rmc))
     to_quad = jnp.exp(-(((NQ - 1 - q) * TOK).astype(F32) * rmc))
@@ -376,27 +362,24 @@
         outb[rows, :] = (loc[rows, :] + add[:, :CD]).astype(BF16)
         outb[rows2, :] = (loc[rows2, :] + add[:, CD:]).astype(BF16)
 
-    arrive(c_gq)
-    base = add_up(gq, NQ)
+    for copy in sent[:-2]:
+        copy.wait()
     total_len = TOK * NQ * NZ * NY
+    load3 = lambda lo, base: lambda i: m3[base + lax.rem(i - yy + NY, NY), lo : lo + 16]
+    p3, _ = pairs(load3(0, 0), load3(16, 0), NY, slab)
+    base = m3[0, 32:40] + m3[1, 32:40] + m3[2, 32:40] + m3[3, 32:40]
     sg_ref[...] = (base[2:3] * (1.0 / math.sqrt(total_len))).reshape(CD)
-    arrive(c_m3)
-
-    def load_y3(lo, base):
-        return lambda i: m3[base + lax.rem(i - yy + NY, NY), lo : lo + 16]
-
-    p3, _ = pairs(load_y3(0, 0), load_y3(16, 0), NY, slab)
-    p4, _ = pairs(load_y3(0, NY), load_y3(16, NY), NY, slab)
-    for k in range(2 * NY):
-        base = base + m3[k, 32:40]
+    arrive(c_o3)
+    p4, _ = pairs(load3(0, NY), load3(16, NY), NY, slab)
+    base = base + m3[4, 32:40] + m3[5, 32:40] + m3[6, 32:40] + m3[7, 32:40]
     grads = fold(unpack(base) + p3 + p4)
     tmp[...] = jnp.zeros_like(tmp)
     tmp[0:MODES, :] = grads
     turned = jnp.transpose(tmp[...])[0:NG, 0:MODES]
     rg_ref[...] = turned * norm * (1.0 / math.sqrt(GROUP * total_len))
 
-    for copy in sent:
-        copy.wait_send()
+    for copy in sent[-2:]:
+        copy.wait()
 
 
 def deliver(a, b, c, to_a, to_b, to_c, sems):
@@ -437,24 +420,23 @@
             pltpu.VMEM((NG * MODES, 2 * BL), F32),
             pltpu.VMEM((NG * MODES, CD), F32),
             pltpu.VMEM((NG * MODES, CD), F32),
+            pltpu.VMEM((NG * MODES, CD), F32),
+            pltpu.VMEM((NG * MODES, CD), F32),
             pltpu.VMEM((NG, BL), F32),
             pltpu.VMEM((NG * MODES, CD), F32),
             pltpu.VMEM((NG, BL, CD), F32),
+            pltpu.VMEM((NG, BL, CD), BF16),
             pltpu.VMEM((TOK, CD), F32),
             pltpu.VMEM((TOK // 2, NG * MODES), BF16),
             pltpu.VMEM((TOK // 2, NG * MODES), BF16),
-            pltpu.VMEM((NQ, MODES, CD), F32),
-            pltpu.VMEM((NQ, MODES, CD), F32),
-            pltpu.VMEM((NZ, MODES, CD), F32),
-            pltpu.VMEM((NZ, 24, CD), F32),
-            pltpu.VMEM((NY, MODES, CD), F32),
+            pltpu.VMEM((NQ, 32, CD), F32),
+            pltpu.VMEM((NZ, 40, CD), F32),
             pltpu.VMEM((2 * NY, 40, CD), F32),
             pltpu.VMEM((NZ, 8, CD), F32),
-            pltpu.VMEM((2 * NY, 8, CD), F32),
             pltpu.VMEM((NQ, 8, CD), F32),
             pltpu.SemaphoreType.DMA((5,)),
-            pltpu.SemaphoreType.DMA((56,)),
-            pltpu.SemaphoreType.DMA((56,)),
+            pltpu.SemaphoreType.DMA((6,)),
+            pltpu.SemaphoreType.DMA((6,)),
         ],
         compiler_params=pltpu.CompilerParams(
             collective_id=0, has_side_effects=True, vmem_limit_bytes=32 << 20

time: 28.8 us -> 27 us (0.938)
  Pallas kernels: 28.1 us -> 26.3 us
    pallas_call x1, Pallas kernels: 27.2 us -> 25.4 us  [shards(): pl.pallas_call(kernel, out_shape=(pltpu.VMEM((TOK, CD), BF16), pltpu.VMEM...]
where the time goes in v4:
time: 27 us; the launch traced here: 26.9 us
  Pallas kernels  26.3 us (97%)
  between operations  0.64 us (2%)
    pallas_call x1, Pallas kernels, shards(): pl.pallas_call(kernel, out_shape=(pltpu.VMEM((TOK, CD), BF16), pltpu.VMEM...  25.4 us
    pallas_call x1, Pallas kernels, shards(): pl.pallas_call(deliver, out_shape=(jax.ShapeDtypeStruct((TOK, CD), BF16),...  0.83 us

profile of v4, /device:TPU:1, one launch (start us, length us, event | category | flops | bytes accessed | tf_op | source)
XLA Modules:
  0.0 26.9 jit_solution(5076426036600111914)
XLA Ops:
  0.6 25.4 %shard_map.76 = (bf16[2048,128]{1,0:T(8,128)(2,1)S(1)}, f32[16,16]{1,0:T(8,128)S(1)}, f32[128]{0:T(128)S(1)}) custom-call(bf16[2048,128]{1,0:T(8,128)(2,1)} %x_hbm.1, bf16[2048,128]{1,0:T(8,128)(2,1)} %y_hbm.1, f32[16,16]{1,0:T(8,128)} %res_hbm.1, f32[16,16]{1,0:T(8,128)} %dec_hbm.1, f32[128]{0:T(128)} %skip_hbm.1), custom_call_target="tpu_custom_call" | custom-call | tf_op jit(solution)/shard_map/pallas_call | solution.py:399
  26.1 0.8 %shard_map.77 = (bf16[2048,128]{1,0:T(8,128)(2,1)}, f32[16,16]{1,0:T(8,128)}, f32[128]{0:T(128)}) custom-call(bf16[2048,128]{1,0:T(8,128)(2,1)S(1)} %get-tuple-element.6.a, f32[16,16]{1,0:T(8,128)S(1)} %get-tuple-element.7.b, f32[128]{0:T(128)S(1)} %get-tuple-element.8.c), custom_call_target="tpu_custom_call" | custom-call | tf_op jit(solution)/shard_map/pallas_call | solution.py:445

commit v5 on v4

--- a/solution.py
+++ b/solution.py
@@ -59,15 +59,31 @@
     )
 
 
-def gather_sum(parts):
-    bit_of = iota(parts[0].shape, 1)
-    for k in (8, 4, 2, 1):
-        keep = (bit_of & k) == 0
-        parts = [
-            jnp.where(keep, low + pltpu.roll(low, CD - k, 1), high + pltpu.roll(high, k, 1))
-            for low, high in zip(parts[:k], parts[k:])
-        ]
-    return parts[0]
+def extract(full):
+    group_of = iota((MODES, CD), 1) % NG
+    out = jnp.zeros((MODES, CD), F32)
+    for g in range(NG):
+        out = jnp.where(group_of == g, full[MODES * g : MODES * (g + 1)], out)
+    return out
+
+
+def swap_dot(bits):
+    row, lane = iota((CD, CD), 0), iota((CD, CD), 1)
+    same = ((row ^ lane) & ~(3 << bits)) == 0
+    row_bits, lane_bits = (row >> bits) & 3, (lane >> bits) & 3
+    return jnp.concatenate(
+        [
+            jnp.concatenate(
+                [
+                    jnp.where(same & (lane_bits == i) & (row_bits == j), 1.0, 0.0).astype(BF16)
+                    for j in range(4)
+                ],
+                axis=1,
+            )
+            for i in range(4)
+        ],
+        axis=0,
+    )
 
 
 def suffix(load_s, count, w):
@@ -102,7 +118,7 @@
 def kernel(
     x_hbm, y_hbm, res_hbm, dec_hbm, skip_hbm,
     outb, rg_ref, sg_ref,
-    x, y, res_ref, dec_ref, skip_ref, xn, yn, tmp, cmc_ref, rates3, pw, pt, ws, wt, zs, tb, lags, after, on, xr, loc, qh, ql,
+    x, y, res_ref, dec_ref, skip_ref, xn, yn, tmp, cmc_ref, rates3, pw, pt, lags, ab, after, on, mid, swap, loc, qh, ql,
     m1, m2, m3, gz, gq,
     load_sem, send_sem, recv_sem,
 ):
@@ -125,16 +141,16 @@
     load_r = pltpu.make_async_copy(res_hbm, res_ref, load_sem.at[2])
     load_d = pltpu.make_async_copy(dec_hbm, dec_ref, load_sem.at[3])
     load_k = pltpu.make_async_copy(skip_hbm, skip_ref, load_sem.at[4])
+    load_d.start()
+    load_y.start()
+    load_x.start()
     barrier = pltpu.get_barrier_semaphore()
     everyone = z_peers + o_peers + y_peers + quad_peers
     for _, peer in everyone:
         pl.semaphore_signal(barrier, inc=1, device_id=peer, device_id_type=MESH)
-    load_d.start()
-    load_y.start()
-    load_x.start()
+
     load_r.start()
     load_k.start()
-
     sent = []
 
     def send(buf, peers, sem):
@@ -155,6 +171,8 @@
     def arrive(copies):
         copies.wait()
 
+    swap[0] = swap_dot(0)
+    swap[1] = swap_dot(2)
     load_d.wait()
     rates = dec_ref[...]
     tmp[...] = jnp.zeros_like(tmp)
@@ -163,72 +181,79 @@
     rmc = jnp.transpose(tmp[...])[:MODES]
     for k in range(3):
         rates3[:, MODES * k : MODES * (k + 1)] = rates
-    span = 2 * BL
-    ahead = iota((MODES, span), 1).astype(F32)
-    behind = span - ahead
-    in_block = (BL * (iota((MODES, CD), 1) % NB)).astype(F32)
-    out_block = float(BL * (NB - 1)) - in_block
+    ahead = iota((MODES, BL), 1).astype(F32)
+    behind = BL - ahead
     for g in range(NG):
-        column = jnp.broadcast_to(rmc[:, g : g + 1], (MODES, span))
+        column = jnp.broadcast_to(rmc[:, g : g + 1], (MODES, BL))
         pw[MODES * g : MODES * (g + 1), :] = jnp.exp(-(column * ahead))
         pt[MODES * g : MODES * (g + 1), :] = jnp.exp(-(column * behind))
-        ws[MODES * g : MODES * (g + 1), :] = jnp.exp(-(column[:, :CD] * in_block))
-        wt[MODES * g : MODES * (g + 1), :] = jnp.exp(-(column[:, :CD] * out_block))
 
     def regroup(src, dst, step):
         for r in range(0, BL, step):
             for g, piece in enumerate(exchange([src[b * BL + r : b * BL + r + step, :] for b in range(NB)])):
                 dst[g, r : r + step, :] = piece
 
+    block_decay = jnp.exp(-(float(BL) * rmc))
+    half_decay = jnp.exp(-(float(TOK // 2) * rmc))
+
+    def block_states(ref, powers):
+        hi, lo = split(powers[...])
+        rates_side = jnp.concatenate([hi, lo], axis=1)
+        states = []
+        for b in range(0, NB, 2):
+            two = jnp.concatenate(
+                [ref[b * BL : (b + 1) * BL, :], ref[(b + 1) * BL : (b + 2) * BL, :]], axis=1
+            )
+            full = nn(rates_side, jnp.concatenate([two, two], axis=0))
+            states += [extract(full[:, :CD]), extract(full[:, CD:])]
+        return states
+
+    load_y.wait()
+    run = jnp.zeros((MODES, CD), F32)
+    behind_block = [None] * NB
+    states = block_states(y, pw)
+    for b in range(NB - 1, -1, -1):
+        behind_block[b] = run
+        ab[b] = run
+        run = states[b] + block_decay * run
+    m1[0, 0:16] = run
+    load_x.wait()
+    states = block_states(x, pt)
+    run = states[0]
+    cross = run * behind_block[0]
+    for b in range(1, NB):
+        cross = cross + states[b] * behind_block[b]
+        run = states[b] + block_decay * run
+    m1[0, 16:32] = run
+
+    for i in range(4):
+        for j in range(4):
+            mid[BL * j : BL * (j + 1), CD * i : CD * (i + 1)] = x[(4 * j + i) * BL : (4 * j + i + 1) * BL, :]
+    part = nn(mid[...], swap[0]).astype(BF16)
+    for i in range(4):
+        for j in range(4):
+            mid[BL * i : BL * (i + 1), CD * j : CD * (j + 1)] = part[BL * j : BL * (j + 1), CD * i : CD * (i + 1)]
+    part = nn(mid[...], swap[1]).astype(BF16)
+    for i in range(4):
+        for j in range(4):
+            xn[4 * j + i] = part[BL * i : BL * (i + 1), CD * j : CD * (j + 1)]
+    regroup(y, yn, 32)
+
+    pl.semaphore_wait(barrier, len(everyone))
+    c_m1 = send(m1, quad_peers, 0)
+    load_r.wait()
+    load_k.wait()
+
     row_c, lane_c = iota((BL, BL), 0), iota((BL, BL), 1)
     flip = jnp.where(lane_c + row_c == BL - 1, 1.0, 0.0).astype(BF16)
-    half_decay = jnp.exp(-(float(TOK // 2) * rmc))
-    load_y.wait()
-    regroup(y, yn, 32)
-    parts = []
     for g in range(NG):
-        gs = slice(MODES * g, MODES * (g + 1))
-        hi, lo = split(pw[gs, :BL])
-        part = nn(jnp.concatenate([hi, lo], axis=0), yn[g])
-        part = part[:MODES] + part[MODES:]
-        zs[gs, :] = part
-        parts.append(part * ws[gs, :])
-    m1[0, 0:16] = gather_sum(parts)
-    load_x.wait()
-    load_r.wait()
-    load_k.wait()
-    regroup(x, xn, 32)
-    parts = []
-    for g in range(NG):
-        gs = slice(MODES * g, MODES * (g + 1))
-        hi, lo = split(pt[gs, BL:])
-        part = nn(jnp.concatenate([flip, hi, lo], axis=0), xn[g])
-        xr[g] = part[:BL].astype(BF16)
-        part = part[BL : BL + MODES] + part[BL + MODES :]
-        tb[gs, :] = part
-        parts.append(part * wt[gs, :])
-    m1[0, 16:32] = gather_sum(parts)
-
-    pl.semaphore_wait(barrier, len(everyone))
-    c_m1 = send(m1, quad_peers, 0)
-
-    for g in range(NG):
-        gram = nt(xr[g], yn[g])
+        gram = nt(nn(flip, xn[g]).astype(BF16), yn[g])
         gram = pltpu.roll(gram, 1, 1, stride=1, stride_axis=0)
         lags[g : g + 1, :] = jnp.sum(jnp.where(lane_c <= row_c, gram, 0.0), axis=0, keepdims=True)
 
-    block_of = iota((NG * MODES, CD), 1) % NB
-    run = zs[...]
-    decay = jnp.broadcast_to(pw[:, BL : BL + 1], (NG * MODES, CD))
-    for k in (1, 2, 4, 8):
-        run = run + jnp.where(block_of + k < NB, decay * pltpu.roll(run, CD - k, 1), 0.0)
-        decay = decay * decay
-    run = jnp.where(block_of + 1 < NB, pltpu.roll(run, CD - 1, 1), 0.0)
-    after[...] = run
-    h = jnp.zeros((MODES, CD), F32)
+    h = cross
     for g in range(NG):
-        gs = slice(MODES * g, MODES * (g + 1))
-        terms = pw[gs, :BL] * lags[g : g + 1, :] + tb[gs, :] * after[gs, :]
+        terms = pw[MODES * g : MODES * (g + 1), :] * lags[g : g + 1, :]
         column = jnp.sum(terms, axis=1, keepdims=True)
         h = h + jnp.where(iota((MODES, CD), 1) == g, column, 0.0)
     skip_sum = jnp.zeros((BL, CD), F32)
@@ -266,7 +291,7 @@
         gs = slice(MODES * g, MODES * (g + 1))
         yq = yn[g]
         column = jnp.broadcast_to(cmc_ref[:, g : g + 1], (MODES, CD))
-        taps = jnp.sum(column * pw[gs, :BL], axis=0, keepdims=True)
+        taps = jnp.sum(column * pw[gs, :], axis=0, keepdims=True)
         toep = pltpu.roll(jnp.broadcast_to(taps, (BL, BL)), 0, 1, stride=1, stride_axis=0)
         th, tl = split(jnp.where(lane_c >= row_c, toep, 0.0))
         ah, al = split(column * after[gs, :])
@@ -277,6 +302,8 @@
             jnp.concatenate([th, tl], axis=1), jnp.concatenate([yq, yq], axis=0)
         ) + nn(reach, jnp.concatenate([ah, ah, al], axis=0))
 
+    for g, piece in enumerate(exchange([ab[b] for b in range(NB)])):
+        after[MODES * g : MODES * (g + 1), :] = piece
     for g in range(NG):
         local_one(g)
 
@@ -416,16 +443,14 @@
             pltpu.VMEM((CD, CD), F32),
             pltpu.VMEM((MODES, CD), F32),
             pltpu.VMEM((NG, 3 * MODES), F32),
-            pltpu.VMEM((NG * MODES, 2 * BL), F32),
-            pltpu.VMEM((NG * MODES, 2 * BL), F32),
-            pltpu.VMEM((NG * MODES, CD), F32),
-            pltpu.VMEM((NG * MODES, CD), F32),
-            pltpu.VMEM((NG * MODES, CD), F32),
-            pltpu.VMEM((NG * MODES, CD), F32),
+            pltpu.VMEM((NG * MODES, BL), F32),
+            pltpu.VMEM((NG * MODES, BL), F32),
             pltpu.VMEM((NG, BL), F32),
+            pltpu.VMEM((NB, MODES, CD), F32),
             pltpu.VMEM((NG * MODES, CD), F32),
             pltpu.VMEM((NG, BL, CD), F32),
-            pltpu.VMEM((NG, BL, CD), BF16),
+            pltpu.VMEM((4 * BL, 4 * CD), BF16),
+            pltpu.VMEM((2, 4 * CD, 4 * CD), BF16),
             pltpu.VMEM((TOK, CD), F32),
             pltpu.VMEM((TOK // 2, NG * MODES), BF16),
             pltpu.VMEM((TOK // 2, NG * MODES), BF16),

time: 27 us -> 26.6 us (0.985)
  Pallas kernels: 26.3 us -> 25.8 us
    pallas_call x1, Pallas kernels: 25.4 us -> 25 us  [shards(): pl.pallas_call(kernel, out_shape=(pltpu.VMEM((TOK, CD), BF16), pltpu.VMEM...]
where the time goes in v5:
time: 26.6 us; the launch traced here: 26.4 us
  Pallas kernels  25.8 us (97%)
  between operations  0.64 us (2%)
    pallas_call x1, Pallas kernels, shards(): pl.pallas_call(kernel, out_shape=(pltpu.VMEM((TOK, CD), BF16), pltpu.VMEM...  25 us
    pallas_call x1, Pallas kernels, shards(): pl.pallas_call(deliver, out_shape=(jax.ShapeDtypeStruct((TOK, CD), BF16),...  0.83 us

profile of v5, /device:TPU:1, one launch (start us, length us, event | category | flops | bytes accessed | tf_op | source)
XLA Modules:
  0.0 26.4 jit_solution(17583932869487077644)
XLA Ops:
  0.6 25.0 %shard_map.76 = (bf16[2048,128]{1,0:T(8,128)(2,1)S(1)}, f32[16,16]{1,0:T(8,128)S(1)}, f32[128]{0:T(128)S(1)}) custom-call(bf16[2048,128]{1,0:T(8,128)(2,1)} %x_hbm.1, bf16[2048,128]{1,0:T(8,128)(2,1)} %y_hbm.1, f32[16,16]{1,0:T(8,128)} %res_hbm.1, f32[16,16]{1,0:T(8,128)} %dec_hbm.1, f32[128]{0:T(128)} %skip_hbm.1), custom_call_target="tpu_custom_call" | custom-call | tf_op jit(solution)/shard_map/pallas_call | solution.py:426
  25.6 0.8 %shard_map.77 = (bf16[2048,128]{1,0:T(8,128)(2,1)}, f32[16,16]{1,0:T(8,128)}, f32[128]{0:T(128)}) custom-call(bf16[2048,128]{1,0:T(8,128)(2,1)S(1)} %get-tuple-element.6.a, f32[16,16]{1,0:T(8,128)S(1)} %get-tuple-element.7.b, f32[128]{0:T(128)S(1)} %get-tuple-element.8.c), custom_call_target="tpu_custom_call" | custom-call | tf_op jit(solution)/shard_map/pallas_call | solution.py:470

commit v6 on v5

--- a/solution.py
+++ b/solution.py
@@ -196,9 +196,15 @@
     block_decay = jnp.exp(-(float(BL) * rmc))
     half_decay = jnp.exp(-(float(TOK // 2) * rmc))
 
-    def block_states(ref, powers):
+    row_c, lane_c = iota((BL, BL), 0), iota((BL, BL), 1)
+    flip = jnp.where(lane_c + row_c == BL - 1, 1.0, 0.0).astype(BF16)
+
+    def block_states(ref, powers, flipped=None):
         hi, lo = split(powers[...])
         rates_side = jnp.concatenate([hi, lo], axis=1)
+        if flipped is not None:
+            flip_side = jnp.concatenate([flip, jnp.zeros_like(flip)], axis=1)
+            rates_side = jnp.concatenate([rates_side, flip_side], axis=0)
         states = []
         for b in range(0, NB, 2):
             two = jnp.concatenate(
@@ -206,6 +212,9 @@
             )
             full = nn(rates_side, jnp.concatenate([two, two], axis=0))
             states += [extract(full[:, :CD]), extract(full[:, CD:])]
+            if flipped is not None:
+                j, i = b // 4, b % 4
+                flipped[BL * j : BL * (j + 1), CD * i : CD * (i + 2)] = full[NG * MODES :].astype(BF16)
         return states
 
     load_y.wait()
@@ -218,7 +227,7 @@
         run = states[b] + block_decay * run
     m1[0, 0:16] = run
     load_x.wait()
-    states = block_states(x, pt)
+    states = block_states(x, pt, mid)
     run = states[0]
     cross = run * behind_block[0]
     for b in range(1, NB):
@@ -226,9 +235,6 @@
         run = states[b] + block_decay * run
     m1[0, 16:32] = run
 
-    for i in range(4):
-        for j in range(4):
-            mid[BL * j : BL * (j + 1), CD * i : CD * (i + 1)] = x[(4 * j + i) * BL : (4 * j + i + 1) * BL, :]
     part = nn(mid[...], swap[0]).astype(BF16)
     for i in range(4):
         for j in range(4):
@@ -244,10 +250,8 @@
     load_r.wait()
     load_k.wait()
 
-    row_c, lane_c = iota((BL, BL), 0), iota((BL, BL), 1)
-    flip = jnp.where(lane_c + row_c == BL - 1, 1.0, 0.0).astype(BF16)
     for g in range(NG):
-        gram = nt(nn(flip, xn[g]).astype(BF16), yn[g])
+        gram = nt(xn[g], yn[g])
         gram = pltpu.roll(gram, 1, 1, stride=1, stride_axis=0)
         lags[g : g + 1, :] = jnp.sum(jnp.where(lane_c <= row_c, gram, 0.0), axis=0, keepdims=True)
 

time: 26.6 us -> 25.9 us (0.974)
  Pallas kernels: 25.8 us -> 25.1 us
    pallas_call x1, Pallas kernels: 25 us -> 24.3 us  [shards(): pl.pallas_call(kernel, out_shape=(pltpu.VMEM((TOK, CD), BF16), pltpu.VMEM...]
where the time goes in v6:
time: 25.9 us; the launch traced here: 25.7 us
  Pallas kernels  25.1 us (97%)
  between operations  0.64 us (2%)
    pallas_call x1, Pallas kernels, shards(): pl.pallas_call(kernel, out_shape=(pltpu.VMEM((TOK, CD), BF16), pltpu.VMEM...  24.3 us
    pallas_call x1, Pallas kernels, shards(): pl.pallas_call(deliver, out_shape=(jax.ShapeDtypeStruct((TOK, CD), BF16),...  0.83 us

profile of v6, /device:TPU:1, one launch (start us, length us, event | category | flops | bytes accessed | tf_op | source)
XLA Modules:
  0.0 25.7 jit_solution(9405875901263155817)
XLA Ops:
  0.6 24.3 %shard_map.76 = (bf16[2048,128]{1,0:T(8,128)(2,1)S(1)}, f32[16,16]{1,0:T(8,128)S(1)}, f32[128]{0:T(128)S(1)}) custom-call(bf16[2048,128]{1,0:T(8,128)(2,1)} %x_hbm.1, bf16[2048,128]{1,0:T(8,128)(2,1)} %y_hbm.1, f32[16,16]{1,0:T(8,128)} %res_hbm.1, f32[16,16]{1,0:T(8,128)} %dec_hbm.1, f32[128]{0:T(128)} %skip_hbm.1), custom_call_target="tpu_custom_call" | custom-call | tf_op jit(solution)/shard_map/pallas_call | solution.py:430
  24.9 0.8 %shard_map.77 = (bf16[2048,128]{1,0:T(8,128)(2,1)}, f32[16,16]{1,0:T(8,128)}, f32[128]{0:T(128)}) custom-call(bf16[2048,128]{1,0:T(8,128)(2,1)S(1)} %get-tuple-element.6.a, f32[16,16]{1,0:T(8,128)S(1)} %get-tuple-element.7.b, f32[128]{0:T(128)S(1)} %get-tuple-element.8.c), custom_call_target="tpu_custom_call" | custom-call | tf_op jit(solution)/shard_map/pallas_call | solution.py:474

commit v7 on v6

--- a/solution.py
+++ b/solution.py
@@ -134,7 +134,8 @@
     quad_peers = [(k, at(yy, z, lax.rem(q + NQ - k, NQ), half)) for k in (2, 3, 1)]
     z_peers = [(k, at(yy, lax.rem(z + NZ - k, NZ), q, half)) for k in (4, 3, 5, 2, 6, 1, 7)]
     y_peers = [(k, at(lax.rem(yy + NY - k, NY), z, q, half)) for k in (2, 1, 3)]
-    o_peers = [(NY + k, at(lax.rem(yy + NY - k, NY), z, q, 1 - half)) for k in (2, 1, 3, 0)]
+    near = lax.rem(q + 2, NQ)
+    o_peers = [(NY + k, at(lax.rem(yy + NY - k, NY), z, near, 1 - half)) for k in (2, 1, 3, 0)]
 
     load_y = pltpu.make_async_copy(y_hbm, y, load_sem.at[0])
     load_x = pltpu.make_async_copy(x_hbm, x, load_sem.at[1])

time: 25.9 us -> 25.6 us (0.988)
  Pallas kernels: 25.1 us -> 24.8 us
    pallas_call x1, Pallas kernels: 24.3 us -> 24 us  [shards(): pl.pallas_call(kernel, out_shape=(pltpu.VMEM((TOK, CD), BF16), pltpu.VMEM...]
where the time goes in v7:
time: 25.6 us; the launch traced here: 25.5 us
  Pallas kernels  24.8 us (97%)
  between operations  0.64 us (2%)
    pallas_call x1, Pallas kernels, shards(): pl.pallas_call(kernel, out_shape=(pltpu.VMEM((TOK, CD), BF16), pltpu.VMEM...  24 us
    pallas_call x1, Pallas kernels, shards(): pl.pallas_call(deliver, out_shape=(jax.ShapeDtypeStruct((TOK, CD), BF16),...  0.83 us

profile of v7, /device:TPU:1, one launch (start us, length us, event | category | flops | bytes accessed | tf_op | source)
XLA Modules:
  0.0 25.5 jit_solution(10454814386998859443)
XLA Ops:
  0.6 24.0 %shard_map.76 = (bf16[2048,128]{1,0:T(8,128)(2,1)S(1)}, f32[16,16]{1,0:T(8,128)S(1)}, f32[128]{0:T(128)S(1)}) custom-call(bf16[2048,128]{1,0:T(8,128)(2,1)} %x_hbm.1, bf16[2048,128]{1,0:T(8,128)(2,1)} %y_hbm.1, f32[16,16]{1,0:T(8,128)} %res_hbm.1, f32[16,16]{1,0:T(8,128)} %dec_hbm.1, f32[128]{0:T(128)} %skip_hbm.1), custom_call_target="tpu_custom_call" | custom-call | tf_op jit(solution)/shard_map/pallas_call | solution.py:431
  24.6 0.8 %shard_map.77 = (bf16[2048,128]{1,0:T(8,128)(2,1)}, f32[16,16]{1,0:T(8,128)}, f32[128]{0:T(128)}) custom-call(bf16[2048,128]{1,0:T(8,128)(2,1)S(1)} %get-tuple-element.6.a, f32[16,16]{1,0:T(8,128)S(1)} %get-tuple-element.7.b, f32[128]{0:T(128)S(1)} %get-tuple-element.8.c), custom_call_target="tpu_custom_call" | custom-call | tf_op jit(solution)/shard_map/pallas_call | solution.py:475

commit v8 on v7

--- a/solution.py
+++ b/solution.py
@@ -154,18 +154,18 @@
     load_k.start()
     sent = []
 
-    def send(buf, peers, sem):
+    def send(buf, peers, sem, rows):
         for slot, peer in peers:
             pltpu.make_async_remote_copy(
-                src_ref=buf.at[0],
-                dst_ref=buf.at[slot],
+                src_ref=buf.at[0, 0:rows],
+                dst_ref=buf.at[slot, 0:rows],
                 send_sem=send_sem.at[sem],
                 recv_sem=recv_sem.at[sem],
                 device_id=peer,
                 device_id_type=MESH,
             ).start()
         slots = [slot for slot, _ in peers]
-        area = buf.at[min(slots) : max(slots) + 1]
+        area = buf.at[min(slots) : max(slots) + 1, 0:rows]
         sent.append(pltpu.make_async_copy(area, area, send_sem.at[sem]))
         return pltpu.make_async_copy(area, area, recv_sem.at[sem])
 
@@ -247,7 +247,7 @@
     regroup(y, yn, 32)
 
     pl.semaphore_wait(barrier, len(everyone))
-    c_m1 = send(m1, quad_peers, 0)
+    c_m1 = send(m1, quad_peers, 0, 32)
     load_r.wait()
     load_k.wait()
 
@@ -267,7 +267,7 @@
         skip_sum = skip_sum + x[rows, :].astype(F32) * y[rows, :].astype(F32)
     skip_sum = jnp.sum(skip_sum, axis=0, keepdims=True)
     gz[0] = pack(h) + jnp.where(iota((8, CD), 0) == 2, skip_sum, 0.0)
-    c_gz = send(gz, z_peers, 1)
+    c_gz = send(gz, z_peers, 1, 8)
 
     dev = jnp.exp(-(float(TOK) * rmc))
     quad = jnp.exp(-(float(TOK * NQ) * rmc))
@@ -278,7 +278,7 @@
     p1, tq = pairs(load1(0), load1(16), NQ, dev)
     m2[0, 16:32] = tq
     m2[0, 32:40] = pack(p1)
-    c_m2 = send(m2, z_peers, 2)
+    c_m2 = send(m2, z_peers, 2, 34)
 
     twice = 2.0 * rates
     series = twice * (1.0 - twice / 2 * (1.0 - twice / 3 * (1.0 - twice / 4 * (
@@ -326,7 +326,7 @@
 
     arrive(c_gz)
     gq[0] = add_up(gz, NZ)
-    c_gq = send(gq, quad_peers, 3)
+    c_gq = send(gq, quad_peers, 3, 8)
 
     hl = TOK // 2
     column = jnp.concatenate(
@@ -345,12 +345,13 @@
     m3[0, 0:16] = suffix(load2(0), NZ, quad)
     p2, ty = pairs(load2(0), load2(16), NZ, quad)
     m3[0, 16:32] = ty
-    lag_part = lag_part + pack(p2)
+    level = lag_part[0:2] + pack(p2)[0:2]
     for k in range(NZ):
-        lag_part = lag_part + m2[k, 32:40]
-    m3[0, 32:40] = lag_part
-    c_o3 = send(m3, o_peers, 4)
-    c_m3 = send(m3, y_peers, 5)
+        level = level + m2[k, 32:34]
+    m3[0, 32:34] = level
+    m3[0, 34:35] = lag_part[2:3]
+    c_o3 = send(m3, o_peers, 4, 35)
+    c_m3 = send(m3, y_peers, 5, 35)
 
     arrive(c_m3)
     one = jnp.ones((MODES, CD), F32)
@@ -399,11 +400,11 @@
     total_len = TOK * NQ * NZ * NY
     load3 = lambda lo, base: lambda i: m3[base + lax.rem(i - yy + NY, NY), lo : lo + 16]
     p3, _ = pairs(load3(0, 0), load3(16, 0), NY, slab)
-    base = m3[0, 32:40] + m3[1, 32:40] + m3[2, 32:40] + m3[3, 32:40]
+    base = m3[0, 32:35] + m3[1, 32:35] + m3[2, 32:35] + m3[3, 32:35]
     sg_ref[...] = (base[2:3] * (1.0 / math.sqrt(total_len))).reshape(CD)
     arrive(c_o3)
     p4, _ = pairs(load3(0, NY), load3(16, NY), NY, slab)
-    base = base + m3[4, 32:40] + m3[5, 32:40] + m3[6, 32:40] + m3[7, 32:40]
+    base = base + m3[4, 32:35] + m3[5, 32:35] + m3[6, 32:35] + m3[7, 32:35]
     grads = fold(unpack(base) + p3 + p4)
     tmp[...] = jnp.zeros_like(tmp)
     tmp[0:MODES, :] = grads

time: 25.6 us -> 25.4 us (level)
  no operation moved by 1% of the time
where the time goes in v8:
time: 25.4 us; the launch traced here: 25.3 us
  Pallas kernels  24.7 us (97%)
  between operations  0.64 us (3%)
    pallas_call x1, Pallas kernels, shards(): pl.pallas_call(kernel, out_shape=(pltpu.VMEM((TOK, CD), BF16), pltpu.VMEM...  23.8 us
    pallas_call x1, Pallas kernels, shards(): pl.pallas_call(deliver, out_shape=(jax.ShapeDtypeStruct((TOK, CD), BF16),...  0.83 us

profile of v8, /device:TPU:1, one launch (start us, length us, event | category | flops | bytes accessed | tf_op | source)
XLA Modules:
  0.0 25.3 jit_solution(6830201736790949623)
XLA Ops:
  0.6 23.8 %shard_map.76 = (bf16[2048,128]{1,0:T(8,128)(2,1)S(1)}, f32[16,16]{1,0:T(8,128)S(1)}, f32[128]{0:T(128)S(1)}) custom-call(bf16[2048,128]{1,0:T(8,128)(2,1)} %x_hbm.1, bf16[2048,128]{1,0:T(8,128)(2,1)} %y_hbm.1, f32[16,16]{1,0:T(8,128)} %res_hbm.1, f32[16,16]{1,0:T(8,128)} %dec_hbm.1, f32[128]{0:T(128)} %skip_hbm.1), custom_call_target="tpu_custom_call" | custom-call | tf_op jit(solution)/shard_map/pallas_call | solution.py:432
  24.5 0.8 %shard_map.77 = (bf16[2048,128]{1,0:T(8,128)(2,1)}, f32[16,16]{1,0:T(8,128)}, f32[128]{0:T(128)}) custom-call(bf16[2048,128]{1,0:T(8,128)(2,1)S(1)} %get-tuple-element.6.a, f32[16,16]{1,0:T(8,128)S(1)} %get-tuple-element.7.b, f32[128]{0:T(128)S(1)} %get-tuple-element.8.c), custom_call_target="tpu_custom_call" | custom-call | tf_op jit(solution)/shard_map/pallas_call | solution.py:476
